TPU v7x, 32 devices: a whole 2x2x4 slice. The times are simulated.
32 devices in a mesh: dp: 2 (over y), row: 4 (over z), col: 4 (over x, core).
Axes of the slice: x: 2, y: 2, z: 4, core: 2. Of those that a mesh axis runs over, the one named last changes fastest.
Arguments:
- tokens_in: bfloat16 [4096, 1536], P(('dp', 'row'), 'col'), may hold values from -6 to 6
- seq_lengths: int32 [2, 4], P('dp'), may hold values from 1 to 1792, 2048 in all within a row
- attention_gain: bfloat16 [1536], P('col'), may hold values from 0.5 to 1.5
- query_weight: bfloat16 [1536, 1536], P('col', 'row'), may hold values from -0.15625 to 0.15625
- query_bias: bfloat16 [1536], P('row'), may hold values from -3 to 3
- keyvalue_weight: bfloat16 [1536, 512], P('col', 'row'), may hold values from -0.15625 to 0.15625
- keyvalue_bias: bfloat16 [512], P('row'), may hold values from -3 to 3
- output_weight: bfloat16 [1536, 1536], P('row', 'col'), may hold values from -0.625 to 0.625
- feedforward_gain: bfloat16 [1536], P('col'), may hold values from 0.5 to 1.5
- gate_weight: bfloat16 [1536, 8960], P('col', 'row'), may hold values from -0.15625 to 0.15625
- up_weight: bfloat16 [1536, 8960], P('col', 'row'), may hold values from -0.15625 to 0.15625
- down_weight: bfloat16 [8960, 1536], P('row', 'col'), may hold values from -0.0625 to 0.0625
- cotangent: bfloat16 [4096, 1536], P(('dp', 'row'), 'col'), may hold values from -6 to 6
Outputs:
- layer_out: bfloat16 [4096, 1536], P(('dp', 'row'), 'col')
- input_grad: bfloat16 [4096, 1536], P(('dp', 'row'), 'col')
- attention_gain_grad: float32 [1536], P('col')
- query_weight_grad: float32 [1536, 1536], P(('col', 'dp'), 'row')
- query_bias_grad: float32 [1536], P(('row', 'dp'))
- keyvalue_weight_grad: float32 [1536, 512], P(('col', 'dp'), 'row')
- keyvalue_bias_grad: float32 [512], P(('row', 'dp'))
- output_weight_grad: float32 [1536, 1536], P(('row', 'dp'), 'col')
- feedforward_gain_grad: float32 [1536], P('col')
- gate_weight_grad: float32 [1536, 8960], P(('col', 'dp'), 'row')
- up_weight_grad: float32 [1536, 8960], P(('col', 'dp'), 'row')
- down_weight_grad: float32 [8960, 1536], P(('row', 'dp'), 'col')
Inputs may be any that keep to these rules, and one draw needn't show every extreme that they name: `seq_lengths`: each row holds the lengths of the 4 sequences of one group in order; a row sums to 2048 and its largest entry is 1792.
All inputs are finite; a program needn't handle non-finite values.
Results may differ from a plain program's by a relative error of at most 0.013.
Values may be sent and summed in bfloat16 or wider, within the bound.
A program may use at most 256 MiB of HBM per device.

v0:
```python
import jax
import jax.numpy as jnp
from jax import lax
from jax.sharding import PartitionSpec as P

D = 1536
HEAD = 128


epsilon = 1e-06
rope_base = 1000000.0
masked_score = -1e30


def partner_2(value, axis, stride):
    mask = 2**stride
    pairs = [(source, source ^ mask) for source in range(lax.axis_size(axis))]
    return lax.ppermute(value, axis, pairs)


def feature_sum(values):
    return lax.psum(jnp.sum(values, axis=-1), "col")


def multiply_by(weight):
    return lambda row_block: jnp.dot(row_block, weight, preferred_element_type=jnp.float32)


def multiply_back(weight):
    return lambda row_block: lax.dot_general(
        row_block, weight, (((1,), (1,)), ((), ())), preferred_element_type=jnp.float32
    )


def outer_sum(left, right):
    return lax.dot_general(
        left, right, (((0,), (0,)), ((), ())), preferred_element_type=jnp.float32
    )


def rows_then_cols(local_block, weight, contract):
    gathered = lax.all_gather(local_block, "row", axis=0, tiled=True)
    result = lax.psum_scatter(
        lax.dot_general(
            gathered, weight, (((1,), (contract,)), ((), ())), preferred_element_type=jnp.float32
        ),
        "col",
        scatter_dimension=0,
        tiled=True,
    )
    return (gathered, result)


def cols_then_rows(local_block, product):
    gathered = lax.all_gather(local_block, "col", axis=0, tiled=True)
    return (gathered, lax.psum_scatter(product(gathered), "row", scatter_dimension=0, tiled=True))


def rotation(positions):
    half_size = HEAD // 2
    inverse_rates = rope_base ** (-jnp.arange(half_size, dtype=jnp.float32) * (2.0 / HEAD))
    angles = positions.astype(jnp.float32)[:, None] * inverse_rates[None, :]
    return (jnp.cos(angles), jnp.sin(angles))


def rotate(values, cosine, sine):
    half_size = HEAD // 2
    shaped = values.reshape(values.shape[0], -1, HEAD)
    first_half = shaped[..., :half_size]
    second_half = shaped[..., half_size:]
    cos_rows = cosine[:, None, :]
    sin_rows = sine[:, None, :]
    turned = jnp.concatenate(
        [
            first_half * cos_rows - second_half * sin_rows,
            second_half * cos_rows + first_half * sin_rows,
        ],
        axis=-1,
    )
    return turned.reshape(values.shape)


def norm_back(grad_normed, normal, inverse, gain):
    scaled = grad_normed * gain
    mean_term = feature_sum(scaled * normal) / D
    grad_rows = inverse[:, None] * (scaled - normal * mean_term[:, None])
    return (grad_rows, jnp.sum(grad_normed * normal, axis=0))


def probabilities(query_block, key_rows, segment_block, place_block, segment, places):
    raw_scores = jnp.einsum(
        "qhd,sd->hqs", query_block, key_rows, preferred_element_type=jnp.float32
    ) * HEAD ** (-0.5)
    allowed = (segment_block[:, None] == segment[None, :]) & (
        places[None, :] <= place_block[:, None]
    )
    masked = jnp.where(allowed[None], raw_scores, masked_score)
    row_top = jnp.max(masked, axis=-1, keepdims=True)
    exponent = jnp.exp(masked - row_top)
    return exponent / jnp.sum(exponent, axis=-1, keepdims=True)


def on_device(
    tokens_in,
    seq_lengths,
    attention_gain,
    query_weight,
    query_bias,
    keyvalue_weight,
    keyvalue_bias,
    output_weight,
    feedforward_gain,
    gate_weight,
    up_weight,
    down_weight,
    cotangent,
):
    group_rows = tokens_in.shape[0] * lax.axis_size("row")
    local_rows = group_rows // lax.axis_size("col")
    places = jnp.arange(group_rows, dtype=jnp.int32)
    lengths_row = seq_lengths[0]
    seq_ends = jnp.cumsum(lengths_row)
    seq_starts = seq_ends - lengths_row
    segment = jnp.sum((places[:, None] >= seq_ends[None, :]).astype(jnp.int32), axis=1)
    owners = segment[:, None] == jnp.arange(lengths_row.shape[0], dtype=jnp.int32)[None, :]
    seq_first = jnp.sum(jnp.where(owners, seq_starts[None, :], 0), axis=1)
    positions = places - seq_first
    col_start = lax.axis_index("col") * local_rows
    local_places = col_start + jnp.arange(local_rows, dtype=jnp.int32)
    local_segment = lax.dynamic_slice_in_dim(segment, col_start, local_rows)
    cosine, sine = rotation(lax.dynamic_slice_in_dim(positions, col_start, local_rows))
    is_key = lax.axis_index("row") % 2 == 0
    inputs = tokens_in.astype(jnp.float32)
    inverse_attn = lax.rsqrt(feature_sum(inputs * inputs) / D + epsilon)
    normal_attn = inputs * inverse_attn[:, None]
    normed = (normal_attn * attention_gain).astype(jnp.bfloat16)
    w_joint = jnp.concatenate([query_weight, keyvalue_weight], axis=1)
    normed_all, joint_pre = rows_then_cols(normed, w_joint, 0)
    width_query = query_weight.shape[1]
    query_pre = joint_pre[:, :width_query] + query_bias
    slot_pre = joint_pre[:, width_query:] + keyvalue_bias
    queries = rotate(query_pre, cosine, sine).astype(jnp.bfloat16)
    own_slot = jnp.where(is_key, rotate(slot_pre, cosine, sine), slot_pre).astype(jnp.bfloat16)
    partner = partner_2(own_slot, "row", 0)
    own_all, partner_all = (
        lax.all_gather(own_slot, "col", axis=0, tiled=True),
        lax.all_gather(partner, "col", axis=0, tiled=True),
    )
    key_rows = jnp.where(is_key, own_all, partner_all)
    value_rows = jnp.where(is_key, partner_all, own_all)
    heads_here = width_query // HEAD
    query_heads = queries.reshape(local_rows, heads_here, HEAD)
    step_rows = min(512, local_rows)
    probs_block = probabilities(query_heads, key_rows, local_segment, local_places, segment, places)
    attended_block = jnp.einsum(
        "hqs,sd->qhd",
        probs_block.astype(jnp.bfloat16),
        value_rows,
        preferred_element_type=jnp.float32,
    )
    outputs = attended_block.reshape(step_rows, width_query)
    attended = outputs.astype(jnp.bfloat16)
    attended_all, branch_attn = cols_then_rows(attended, multiply_by(output_weight))
    middle = inputs + branch_attn
    inverse_mlp = lax.rsqrt(feature_sum(middle * middle) / D + epsilon)
    normal_mlp = middle * inverse_mlp[:, None]
    normed_mlp = (normal_mlp * feedforward_gain).astype(jnp.bfloat16)
    w_pair = jnp.concatenate([gate_weight, up_weight], axis=1)
    normed_mlp_all, gate_up = rows_then_cols(normed_mlp, w_pair, 0)
    width_ff = gate_weight.shape[1]
    gate_act = gate_up[:, :width_ff]
    up_act = gate_up[:, width_ff:]
    hidden = (jax.nn.silu(gate_act) * up_act).astype(jnp.bfloat16)
    hidden_all, branch_mlp = cols_then_rows(hidden, multiply_by(down_weight))
    layer_out = (middle + branch_mlp).astype(jnp.bfloat16)
    grad_out = cotangent.astype(jnp.float32)
    grad_out_all, grad_hidden = rows_then_cols(cotangent, down_weight, 1)
    hidden_kept = lax.all_gather(hidden, "col", axis=0, tiled=True)
    grad_w_down = outer_sum(hidden_kept, grad_out_all)
    gate_sigmoid = jax.nn.sigmoid(gate_act)
    grad_gate = grad_hidden * up_act * gate_sigmoid * (1.0 + gate_act * (1.0 - gate_sigmoid))
    grad_up = grad_hidden * (gate_act * gate_sigmoid)
    grad_pair = jnp.concatenate([grad_gate, grad_up], axis=1).astype(jnp.bfloat16)
    grad_pair_all, grad_normed_mlp = cols_then_rows(grad_pair, multiply_back(w_pair))
    grad_w_pair = outer_sum(normed_mlp_all, grad_pair_all)
    grad_middle_norm, mlp_gain_part = norm_back(
        grad_normed_mlp, normal_mlp, inverse_mlp, feedforward_gain
    )
    grad_middle = grad_out + grad_middle_norm
    grad_middle_all, grad_attended = rows_then_cols(
        grad_middle.astype(jnp.bfloat16), output_weight, 1
    )
    grad_w_out = outer_sum(attended_all, grad_middle_all)
    grad_heads = grad_attended.astype(jnp.bfloat16).reshape(local_rows, heads_here, HEAD)
    score_scale = HEAD ** (-0.5)
    probs_block = probabilities(query_heads, key_rows, local_segment, local_places, segment, places)
    grad_values = jnp.einsum(
        "hqs,qhd->sd",
        probs_block.astype(jnp.bfloat16),
        grad_heads,
        preferred_element_type=jnp.float32,
    )
    grad_probs = jnp.einsum(
        "qhd,sd->hqs", grad_heads, value_rows, preferred_element_type=jnp.float32
    )
    grad_scores = probs_block * (
        grad_probs - jnp.sum(probs_block * grad_probs, axis=-1, keepdims=True)
    )
    grad_low = grad_scores.astype(jnp.bfloat16)
    grad_query_block = (
        jnp.einsum("hqs,sd->qhd", grad_low, key_rows, preferred_element_type=jnp.float32)
        * score_scale
    )
    grad_keys = (
        jnp.einsum("hqs,qhd->sd", grad_low, query_heads, preferred_element_type=jnp.float32)
        * score_scale
    )
    query_grads = grad_query_block.reshape(step_rows, width_query)
    key_share, value_share = (
        lax.psum_scatter(grad_keys, "col", scatter_dimension=0, tiled=True),
        lax.psum_scatter(grad_values, "col", scatter_dimension=0, tiled=True),
    )
    outgoing = jnp.where(is_key, value_share, key_share)
    incoming = partner_2(outgoing, "row", 0)
    grad_slot = jnp.where(is_key, key_share, value_share) + incoming
    grad_slot_pre = jnp.where(is_key, rotate(grad_slot, cosine, -sine), grad_slot)
    grad_query_pre = rotate(query_grads, cosine, -sine)
    grad_joint = jnp.concatenate([grad_query_pre, grad_slot_pre], axis=1).astype(jnp.bfloat16)
    grad_joint_all, grad_normed = cols_then_rows(grad_joint, multiply_back(w_joint))
    grad_w_joint = outer_sum(normed_all, grad_joint_all)
    grad_bias = jnp.sum(grad_joint_all.astype(jnp.float32), axis=0)
    grad_inputs_norm, attn_gain_part = norm_back(
        grad_normed, normal_attn, inverse_attn, attention_gain
    )
    input_grad = (grad_middle + grad_inputs_norm).astype(jnp.bfloat16)
    summed = (
        lax.psum_scatter(grad_w_joint[:, :width_query], "dp", scatter_dimension=0, tiled=True),
        lax.psum_scatter(grad_bias[:width_query], "dp", scatter_dimension=0, tiled=True),
        lax.psum_scatter(grad_w_joint[:, width_query:], "dp", scatter_dimension=0, tiled=True),
        lax.psum_scatter(grad_bias[width_query:], "dp", scatter_dimension=0, tiled=True),
        lax.psum_scatter(grad_w_out, "dp", scatter_dimension=0, tiled=True),
        lax.psum_scatter(grad_w_pair[:, :width_ff], "dp", scatter_dimension=0, tiled=True),
        lax.psum_scatter(grad_w_pair[:, width_ff:], "dp", scatter_dimension=0, tiled=True),
        lax.psum_scatter(grad_w_down, "dp", scatter_dimension=0, tiled=True),
    )
    gain_sums = lax.psum((attn_gain_part, mlp_gain_part), ("dp", "row"))
    return (
        layer_out,
        input_grad,
        gain_sums[0],
        summed[0],
        summed[1],
        summed[2],
        summed[3],
        summed[4],
        gain_sums[1],
        summed[5],
        summed[6],
        summed[7],
    )


def solution(mesh):
    return jax.shard_map(
        on_device,
        mesh=mesh,
        in_specs=(
            P(("dp", "row"), "col"),
            P("dp", None),
            P("col"),
            P("col", "row"),
            P("row"),
            P("col", "row"),
            P("row"),
            P("row", "col"),
            P("col"),
            P("col", "row"),
            P("col", "row"),
            P("row", "col"),
            P(("dp", "row"), "col"),
        ),
        out_specs=(
            P(("dp", "row"), "col"),
            P(("dp", "row"), "col"),
            P("col"),
            P(("col", "dp"), "row"),
            P(("row", "dp")),
            P(("col", "dp"), "row"),
            P(("row", "dp")),
            P(("row", "dp"), "col"),
            P("col"),
            P(("col", "dp"), "row"),
            P(("col", "dp"), "row"),
            P(("row", "dp"), "col"),
        ),
        check_vma=False,
    )
```

profile of v0, /device:TPU:0, one launch (start us, length us, event | category | flops | bytes accessed | tf_op | source)
XLA Modules:
  0.0 1519.3 jit_solution(11237557333913685519)
XLA Ops:
  22.0 35.6 %all-gather.9.cloned.1.call-done = bf16[2048,384]{1,0:T(8,128)(2,1)} async-done(((bf16[512,384]{1,0:T(8,128)(2,1)}), bf16[2048,384]{1,0:T(8,128)(2,1)}) %all-gather.9.cloned.1.call-update) | async-done | bytes 1572880 | tf_op jit(solution)/shard_map/all_gather | solution.py:42
  67.0 38.8 %reduce-scatter.17.cloned.1.call-done = f32[512,512]{1,0:T(8,128)} async-done(((f32[2048,512]{1,0:T(8,128)}), f32[512,512]{1,0:T(8,128)}) %reduce-scatter.17.cloned.1.call-update) | async-done | bytes 1048592 | tf_op jit(solution)/shard_map/reduce_scatter | solution.py:43
  131.3 11.2 fusion.74
  149.5 19.0 %all-gather.11.cloned.1.call-done = bf16[2048,384]{0,1:T(8,128)(2,1)} async-done(((bf16[512,384]{0,1:T(8,128)(2,1)}), bf16[2048,384]{0,1:T(8,128)(2,1)}) %all-gather.11.cloned.1.call-update) | async-done | bytes 1572880 | tf_op jit(solution)/shard_map/all_gather | solution.py:55
  173.4 59.8 %reduce-scatter.19.cloned.1.call-done = f32[512,384]{1,0:T(8,128)} async-done(((f32[2048,384]{1,0:T(8,128)}), f32[512,384]{1,0:T(8,128)}) %reduce-scatter.19.cloned.1.call-update) | async-done | bytes 786448 | tf_op jit(solution)/shard_map/reduce_scatter | solution.py:56
  241.9 29.9 %all-gather.17.cloned.1.call-done = bf16[2048,384]{1,0:T(8,128)(2,1)} async-done(((bf16[512,384]{1,0:T(8,128)(2,1)}), bf16[2048,384]{1,0:T(8,128)(2,1)}) %all-gather.17.cloned.1.call-update) | async-done | bytes 1572880 | tf_op jit(solution)/shard_map/all_gather | solution.py:42
  271.8 10.9 fusion.83
  287.2 22.7 %all-gather.13.cloned.1.call-done = bf16[2048,384]{1,0:T(8,128)(2,1)} async-done(((bf16[512,384]{1,0:T(8,128)(2,1)}), bf16[2048,384]{1,0:T(8,128)(2,1)}) %all-gather.13.cloned.1.call-update) | async-done | bytes 1572880 | tf_op jit(solution)/shard_map/all_gather | solution.py:42
  309.9 27.3 %fusion.81 = f32[2048,4480]{1,0:T(8,128)} fusion(bf16[2048,384]{1,0:T(8,128)(2,1)} %all-gather.13.cloned.1.call-done, bf16[384,4480]{0,1:T(8,128)(2,1)} %constant_dynamic-update-slice_fusion.2), kind=kOutput, calls=%fused_computation.126 | convolution fusion | flops 7046430720 | bytes 41713664 | tf_op jit(solution)/shard_map/dot_general | solution.py:44
  337.3 113.8 %reduce-scatter.25.cloned.1.call-done = f32[512,2240]{1,0:T(8,128)} async-done(((f32[2048,2240]{1,0:T(8,128)}), f32[512,2240]{1,0:T(8,128)}) %reduce-scatter.25.cloned.1.call-update) | async-done | bytes 4587536 | tf_op jit(solution)/shard_map/reduce_scatter | solution.py:43
  451.0 257.4 %reduce-scatter.21.cloned.1.call-done = f32[512,4480]{1,0:T(8,128)} async-done(((f32[2048,4480]{1,0:T(8,128)}), f32[512,4480]{1,0:T(8,128)}) %reduce-scatter.21.cloned.1.call-update) | async-done | bytes 9175056 | tf_op jit(solution)/shard_map/reduce_scatter | solution.py:43
  719.6 117.0 %all-gather.19.cloned.1.call-done = bf16[2048,4480]{1,0:T(8,128)(2,1)} async-done(((bf16[512,4480]{1,0:T(8,128)(2,1)}), bf16[2048,4480]{1,0:T(8,128)(2,1)}) %all-gather.19.cloned.1.call-update) | async-done | bytes 18350096 | tf_op jit(solution)/shard_map/all_gather | solution.py:55
  836.6 15.6 %fusion.84 = f32[2048,384]{1,0:T(8,128)} fusion(bf16[2048,4480]{1,0:T(8,128)(2,1)} %all-gather.19.cloned.1.call-done, bf16[384,4480]{0,1:T(8,128)(2,1)} %constant_dynamic-update-slice_fusion.2), kind=kOutput, calls=%fused_computation.129 | convolution fusion | flops 7046430720 | bytes 24936448 | tf_op jit(solution)/shard_map/dot_general | solution.py:30
  852.3 60.4 %reduce-scatter.27.cloned.1.call-done = f32[512,384]{1,0:T(8,128)} async-done(((f32[2048,384]{1,0:T(8,128)}), f32[512,384]{1,0:T(8,128)}) %reduce-scatter.27.cloned.1.call-update) | async-done | bytes 786448 | tf_op jit(solution)/shard_map/reduce_scatter | solution.py:56
  923.8 36.8 %all-gather.21.cloned.1.call-done = bf16[2048,384]{1,0:T(8,128)(2,1)} async-done(((bf16[512,384]{1,0:T(8,128)(2,1)}), bf16[2048,384]{1,0:T(8,128)(2,1)}) %all-gather.21.cloned.1.call-update) | async-done | bytes 1572880 | tf_op jit(solution)/shard_map/all_gather | solution.py:42
  964.9 36.9 %reduce-scatter.29.cloned.1.call-done = f32[512,384]{1,0:T(8,128)} async-done(((f32[2048,384]{1,0:T(8,128)}), f32[512,384]{1,0:T(8,128)}) %reduce-scatter.29.cloned.1.call-update) | async-done | bytes 786448 | tf_op jit(solution)/shard_map/reduce_scatter | solution.py:43
  1003.9 11.8 fusion.1
  1041.4 11.6 reduce-scatter.31.cloned.1.call-done
  1053.0 28.1 %reduce-scatter.33.cloned.1.call-done = f32[512,128]{1,0:T(8,128)} async-done(((f32[2048,128]{1,0:T(8,128)}), f32[512,128]{1,0:T(8,128)}) %reduce-scatter.33.cloned.1.call-update) | async-done | bytes 262160 | tf_op jit(solution)/shard_map/reduce_scatter | solution.py:221
  1098.2 22.3 %all-gather.23.cloned.1.call-done = bf16[2048,512]{0,1:T(8,128)(2,1)} async-done(((bf16[512,512]{0,1:T(8,128)(2,1)}), bf16[2048,512]{0,1:T(8,128)(2,1)}) %all-gather.23.cloned.1.call-update) | async-done | bytes 2097168 | tf_op jit(solution)/shard_map/all_gather | solution.py:55
  1125.1 61.1 %all-gather.15.cloned.1.call-done = bf16[2048,2240]{1,0:T(8,128)(2,1)} async-done(((bf16[512,2240]{1,0:T(8,128)(2,1)}), bf16[2048,2240]{1,0:T(8,128)(2,1)}) %all-gather.15.cloned.1.call-update) | async-done | bytes 9175056 | tf_op jit(solution)/shard_map/all_gather | solution.py:55
  1186.2 9.1 fusion.82
  1195.4 10.9 fusion.90
  1206.7 11.2 fusion.89
  1250.1 21.6 %all-reduce.2 = (f32[384]{0:T(512)}, f32[384]{0:T(512)}) all-reduce(f32[384]{0:T(512)S(1)} %get-tuple-element.14, f32[384]{0:T(512)S(1)} %copy-done.28), channel_id=1, replica_groups=mesh['dp'=2,'row'=4,'col'=4] {'dp','row'}, use_global_device_ids=true, to_apply=%region_25.26 | all-reduce | flops 768 | bytes 6144 | tf_op jit(solution)/shard_map/psum | solution.py:246
  1277.8 33.6 %reduce-scatter.23.cloned.1.call-done = f32[512,384]{1,0:T(8,128)} async-done(((f32[2048,384]{1,0:T(8,128)}), f32[512,384]{1,0:T(8,128)}) %reduce-scatter.23.cloned.1.call-update) | async-done | bytes 786448 | tf_op jit(solution)/shard_map/reduce_scatter | solution.py:56
  1314.3 46.6 %reduce-scatter.47.cloned.1.call-done = f32[1120,384]{1,0:T(8,128)} async-done(((f32[2240,384]{1,0:T(8,128)}), f32[1120,384]{1,0:T(8,128)}) %reduce-scatter.47.cloned.1.call-update) | async-done | bytes 1720336 | tf_op jit(solution)/shard_map/reduce_scatter | solution.py:244
  1360.9 50.3 %reduce-scatter.43.cloned.1.call-done = f32[192,2240]{1,0:T(8,128)} async-done(((f32[384,2240]{1,0:T(8,128)}), f32[192,2240]{1,0:T(8,128)}) %reduce-scatter.43.cloned.1.call-update) | async-done | bytes 1720336 | tf_op jit(solution)/shard_map/reduce_scatter | solution.py:242
  1411.2 50.6 %reduce-scatter.45.cloned.1.call-done = f32[192,2240]{1,0:T(8,128)} async-done(((f32[384,2240]{1,0:T(8,128)}), f32[192,2240]{1,0:T(8,128)}) %reduce-scatter.45.cloned.1.call-update) | async-done | bytes 1720336 | tf_op jit(solution)/shard_map/reduce_scatter | solution.py:243
  1461.9 18.2 %reduce-scatter.41.cloned.1.call-done = f32[192,384]{1,0:T(8,128)} async-done(((f32[384,384]{1,0:T(8,128)}), f32[192,384]{1,0:T(8,128)}) %reduce-scatter.41.cloned.1.call-update) | async-done | bytes 294928 | tf_op jit(solution)/shard_map/reduce_scatter | solution.py:241
  1480.0 13.8 reduce-scatter.39.cloned.1.call-done
  1493.9 18.1 %reduce-scatter.37.cloned.1.call-done = f32[192,384]{1,0:T(8,128)} async-done(((f32[384,384]{1,0:T(8,128)}), f32[192,384]{1,0:T(8,128)}) %reduce-scatter.37.cloned.1.call-update) | async-done | bytes 294928 | tf_op jit(solution)/shard_map/reduce_scatter | solution.py:237
  (209 shorter events, 190.7 us)
Async XLA Ops:
  7.2 264.6 %copy-start = (bf16[2240,384]{1,0:T(8,128)(2,1)S(1)}, bf16[2240,384]{1,0:T(8,128)(2,1)}, u32[]{:S(2)}) copy-start(bf16[2240,384]{1,0:T(8,128)(2,1)} %param.24) | copy-start | bytes 5160964
  7.2 50.4 %all-gather.9.cloned.1.call-start = ((), (), s32[]{:S(2)}) async-start(), calls=%async_computation.16 | async-start | bytes 1966080 | tf_op jit(solution)/shard_map/all_gather | solution.py:42
  20.0 85.7 %reduce-scatter.17.cloned.1.call-start = ((), (), s32[]{:S(2)}) async-start(), calls=%async_computation.17 | async-start | bytes 5242880 | tf_op jit(solution)/shard_map/reduce_scatter | solution.py:43
  62.2 106.3 %all-gather.11.cloned.1.call-start = ((), (), s32[]{:S(2)}) async-start(), calls=%async_computation.18 | async-start | bytes 1966080 | tf_op jit(solution)/shard_map/all_gather | solution.py:55
  109.6 14.1 collective-permute-start
  149.0 84.2 %copy-start.2 = (bf16[512,384]{1,0:T(8,128)(2,1)S(1)}, bf16[512,384]{1,0:T(8,128)(2,1)}, u32[]{:S(2)}) copy-start(bf16[512,384]{1,0:T(8,128)(2,1)} %param.13) | copy-start | bytes 1179652
  149.0 84.2 %reduce-scatter.19.cloned.1.call-start = ((), (), s32[]{:S(2)}) async-start(), calls=%async_computation.19 | async-start | bytes 3932160 | tf_op jit(solution)/shard_map/reduce_scatter | solution.py:56
  172.8 99.1 %all-gather.17.cloned.1.call-start = ((), (), s32[]{:S(2)}) async-start(), calls=%async_computation.24 | async-start | bytes 1966080 | tf_op jit(solution)/shard_map/all_gather | solution.py:42
  173.4 136.5 %all-gather.13.cloned.1.call-start = ((), (), s32[]{:S(2)}) async-start(), calls=%async_computation.20 | async-start | bytes 1966080 | tf_op jit(solution)/shard_map/all_gather | solution.py:42
  173.4 747.7 %copy-start.17 = (f32[384]{0:T(512)}, f32[384]{0:T(512)S(1)}, u32[]{:S(2)}) copy-start(f32[384]{0:T(512)S(1)} %convert_element_type.85) | copy-start | bytes 4612
  240.9 680.2 %copy-start.19 = (f32[512]{0:T(512)}, f32[512]{0:T(512)S(1)}, u32[]{:S(2)}) copy-start(f32[512]{0:T(512)S(1)} %add_rsqrt_fusion) | copy-start | bytes 6148
  241.8 209.2 %reduce-scatter.25.cloned.1.call-start = ((), (), s32[]{:S(2)}) async-start(), calls=%async_computation.25 | async-start | bytes 23592960 | tf_op jit(solution)/shard_map/reduce_scatter | solution.py:43
  282.8 425.7 %reduce-scatter.21.cloned.1.call-start = ((), (), s32[]{:S(2)}) async-start(), calls=%async_computation.21 | async-start | bytes 45875200 | tf_op jit(solution)/shard_map/reduce_scatter | solution.py:43
  337.2 499.4 %all-gather.19.cloned.1.call-start = ((), (), s32[]{:S(2)}) async-start(), calls=%async_computation.26 | async-start | bytes 22937600 | tf_op jit(solution)/shard_map/all_gather | solution.py:55
  719.3 193.4 %reduce-scatter.27.cloned.1.call-start = ((), (), s32[]{:S(2)}) async-start(), calls=%async_computation.27 | async-start | bytes 3932160 | tf_op jit(solution)/shard_map/reduce_scatter | solution.py:56
  852.3 108.3 %all-gather.21.cloned.1.call-start = ((), (), s32[]{:S(2)}) async-start(), calls=%async_computation.28 | async-start | bytes 1966080 | tf_op jit(solution)/shard_map/all_gather | solution.py:42
  923.8 78.0 %reduce-scatter.29.cloned.1.call-start = ((), (), s32[]{:S(2)}) async-start(), calls=%async_computation.29 | async-start | bytes 3932160 | tf_op jit(solution)/shard_map/reduce_scatter | solution.py:43
  964.9 88.1 %reduce-scatter.31.cloned.1.call-start = ((), (), s32[]{:S(2)}) async-start(), calls=%async_computation.30 | async-start | bytes 1310720 | tf_op jit(solution)/shard_map/reduce_scatter | solution.py:220
  1028.1 52.9 %reduce-scatter.33.cloned.1.call-start = ((), (), s32[]{:S(2)}) async-start(), calls=%async_computation.31 | async-start | bytes 1310720 | tf_op jit(solution)/shard_map/reduce_scatter | solution.py:221
  1035.5 85.0 %all-gather.23.cloned.1.call-start = ((), (), s32[]{:S(2)}) async-start(), calls=%async_computation.32 | async-start | bytes 2621440 | tf_op jit(solution)/shard_map/all_gather | solution.py:55
  1082.7 8.4 collective-permute-start.1
  1097.6 88.6 %all-gather.15.cloned.1.call-start = ((), (), s32[]{:S(2)}) async-start(), calls=%async_computation.22 | async-start | bytes 11796480 | tf_op jit(solution)/shard_map/all_gather | solution.py:55
  1098.2 150.4 %reduce-scatter.35.cloned.1.call-start = ((), (), s32[]{:S(2)}) async-start(), calls=%async_computation.33 | async-start | bytes 3932160 | tf_op jit(solution)/shard_map/reduce_scatter | solution.py:56
  1125.1 186.3 %reduce-scatter.23.cloned.1.call-start = ((), (), s32[]{:S(2)}) async-start(), calls=%async_computation.23 | async-start | bytes 3932160 | tf_op jit(solution)/shard_map/reduce_scatter | solution.py:56
  1195.4 165.5 %reduce-scatter.47.cloned.1.call-start = ((), (), s32[]{:S(2)}) async-start(), calls=%async_computation.39 | async-start | bytes 5160960 | tf_op jit(solution)/shard_map/reduce_scatter | solution.py:244
  1206.4 204.9 %reduce-scatter.43.cloned.1.call-start = ((), (), s32[]{:S(2)}) async-start(), calls=%async_computation.37 | async-start | bytes 5308416 | tf_op jit(solution)/shard_map/reduce_scatter | solution.py:242
  1222.0 239.9 %reduce-scatter.45.cloned.1.call-start = ((), (), s32[]{:S(2)}) async-start(), calls=%async_computation.38 | async-start | bytes 5308416 | tf_op jit(solution)/shard_map/reduce_scatter | solution.py:243
  1222.7 257.3 %reduce-scatter.41.cloned.1.call-start = ((), (), s32[]{:S(2)}) async-start(), calls=%async_computation.36 | async-start | bytes 884736 | tf_op jit(solution)/shard_map/reduce_scatter | solution.py:241
  1226.5 267.4 %reduce-scatter.39.cloned.1.call-start = ((), (), s32[]{:S(2)}) async-start(), calls=%async_computation.35 | async-start | bytes 294912 | tf_op jit(solution)/shard_map/reduce_scatter | solution.py:239
  1230.6 80.8 %copy-start.18 = (f32[384]{0:T(512)S(1)}, f32[384]{0:T(512)}, u32[]{:S(2)}) copy-start(f32[384]{0:T(512)} %copy-done.17) | copy-start | bytes 4612
  1230.6 80.8 %copy-start.20 = (f32[512]{0:T(512)S(1)}, f32[512]{0:T(512)}, u32[]{:S(2)}) copy-start(f32[512]{0:T(512)} %copy-done.19) | copy-start | bytes 6148
  1231.3 280.7 %reduce-scatter.37.cloned.1.call-start = ((), (), s32[]{:S(2)}) async-start(), calls=%async_computation.34 | async-start | bytes 884736 | tf_op jit(solution)/shard_map/reduce_scatter | solution.py:237
  (32 other events, 696.4 us)
Sparse Core Ops, SparseCore 0:
  20.1 37.4 all-gather.8
  62.3 43.3 reduce-scatter.16
  149.1 19.3 all-gather.10
  172.9 60.2 reduce-scatter.18
  234.7 37.0 all-gather.16
  273.9 35.9 all-gather.12
  312.7 138.3 reduce-scatter.24
  453.7 254.7 reduce-scatter.20
  719.5 117.1 all-gather.18
  852.4 60.2 reduce-scatter.26
  923.9 36.6 all-gather.20
  965.0 36.7 reduce-scatter.28
  1028.2 24.7 reduce-scatter.30
  1056.1 24.8 reduce-scatter.32
  1097.7 22.7 all-gather.22
  1121.9 64.2 all-gather.14
  1188.3 60.2 reduce-scatter.34
  1250.8 60.5 reduce-scatter.22
  1314.2 46.6 reduce-scatter.46
  1363.6 47.6 reduce-scatter.42
  1414.2 47.6 reduce-scatter.44
  1464.7 15.2 reduce-scatter.40
  1482.9 10.9 reduce-scatter.38
  1496.7 15.2 reduce-scatter.36
where the time goes:
time: 1530 us; the launch traced here: 1520 us
  waiting for transfers between devices  1190 us (78%)
  matrix products  155 us (10%)
  blocking collectives  67.9 us (4%)
  other arithmetic  56.2 us (4%)
  local copies, waits for them, and re-layouts  25.9 us (2%)
  between operations  16.6 us (1%)
    reduce_scatter x4, waiting for transfers between devices, rows_then_cols(): lax.psum_scatter(lax.dot_general(gathered, weight, (((1,), (contract,)),...  447 us
    all_gather x4, waiting for transfers between devices, cols_then_rows(): gathered = lax.all_gather(local_block, 'col', axis=0, tiled=True)  219 us
    reduce_scatter x4, waiting for transfers between devices, cols_then_rows(): lax.psum_scatter(product(gathered), 'row', scatter_dimension=0, tiled=True)  159 us
    all_gather x4, waiting for transfers between devices, rows_then_cols(): gathered = lax.all_gather(local_block, 'row', axis=0, tiled=True)  125 us
    reduce_scatter x1, waiting for transfers between devices, on_device(): lax.psum_scatter(grad_w_pair[:, width_ff:], 'dp', scatter_dimension=0, ti...  50.6 us
    reduce_scatter x1, waiting for transfers between devices, on_device(): lax.psum_scatter(grad_w_pair[:, :width_ff], 'dp', scatter_dimension=0, ti...  50.3 us
    dot_general x4, matrix products, rows_then_cols(): lax.dot_general(gathered, weight, (((1,), (contract,)), ((), ())), prefer...  47 us
    reduce_scatter x1, waiting for transfers between devices, on_device(): lax.psum_scatter(grad_w_down, 'dp', scatter_dimension=0, tiled=True)  46.6 us
  transfers between devices with their start and end apart: 26, of which 25 were waited for; matrix products, arithmetic and copies ran while one was open for 9% of the time, Pallas kernels for 0%

commit v1 on v0

v1 whole, which is shorter than its diff:
```python
import jax
import jax.numpy as jnp
from jax import lax
from jax.sharding import PartitionSpec as P

HEAD = 128
epsilon = 1e-06
rope_base = 1000000.0
masked_score = -1e30
BF = jnp.bfloat16
F32 = jnp.float32


def dot(a, b, ca=1, cb=0):
    return lax.dot_general(a, b, (((ca,), (cb,)), ((), ())), preferred_element_type=F32)


def partner(value, axis, mask):
    pairs = [(s, s ^ mask) for s in range(lax.axis_size(axis))]
    return lax.ppermute(value, axis, pairs)


def gather(value, axis, dim=0):
    return lax.all_gather(value, axis, axis=dim, tiled=True)


def scatter_sum(value, axis, dim=0):
    return lax.psum_scatter(value.astype(BF), axis, scatter_dimension=dim, tiled=True)


def features_to_tokens(block):
    cols = lax.axis_size("col")
    sub = block.shape[0] // cols
    out = lax.all_to_all(block.reshape(cols, sub, -1), "col", 0, 0, tiled=True)
    return jnp.moveaxis(out, 0, 1).reshape(sub, -1)


def tokens_to_features(block):
    cols = lax.axis_size("col")
    sub = block.shape[0]
    parts = jnp.moveaxis(block.reshape(sub, cols, -1), 1, 0)
    out = lax.all_to_all(parts, "col", 0, 0, tiled=True)
    return out.reshape(cols * sub, -1)


def rotation(positions):
    half = HEAD // 2
    rates = rope_base ** (-jnp.arange(half, dtype=F32) * (2.0 / HEAD))
    angles = positions.astype(F32)[:, None] * rates[None, :]
    return jnp.cos(angles), jnp.sin(angles)


def rotate(values, cosine, sine):
    half = HEAD // 2
    shaped = values.reshape(values.shape[0], -1, HEAD)
    a, b = shaped[..., :half], shaped[..., half:]
    c, s = cosine[:, None, :], sine[:, None, :]
    turned = jnp.concatenate([a * c - b * s, b * c + a * s], axis=-1)
    return turned.reshape(values.shape)


def norm_back(grad, normal, inverse, gain):
    e = grad * gain
    mean = jnp.mean(e * normal, axis=-1, keepdims=True)
    return inverse * (e - normal * mean), jnp.sum(grad * normal, axis=0)


def on_device(
    tokens_in, seq_lengths, attention_gain, query_weight, query_bias, keyvalue_weight,
    keyvalue_bias, output_weight, feedforward_gain, gate_weight, up_weight, down_weight,
    cotangent,
):
    rows, cols = lax.axis_size("row"), lax.axis_size("col")
    col = lax.axis_index("col")
    row_tokens = tokens_in.shape[0]
    group = row_tokens * rows
    sub = row_tokens // cols
    wq_width = query_weight.shape[1]
    heads = wq_width // HEAD
    is_key = lax.axis_index("row") % 2 == 0
    places = jnp.arange(group, dtype=jnp.int32)
    lengths = seq_lengths[0]
    ends = jnp.cumsum(lengths)
    segment = jnp.sum((places[:, None] >= ends[None, :]).astype(jnp.int32), axis=1)
    owners = segment[:, None] == jnp.arange(lengths.shape[0], dtype=jnp.int32)[None, :]
    first = jnp.sum(jnp.where(owners, (ends - lengths)[None, :], 0), axis=1)
    positions = places - first
    own = lambda v: lax.dynamic_slice_in_dim(v.reshape(rows, cols, sub), col, 1, 1).reshape(-1)
    my_places, my_segment, my_positions = own(places), own(segment), own(positions)
    cosine, sine = rotation(my_positions)
    mate = partner(keyvalue_weight, "row", 1)
    mate_bias = partner(keyvalue_bias, "row", 1)
    key_w = jnp.where(is_key, keyvalue_weight, mate)
    value_w = jnp.where(is_key, mate, keyvalue_weight)
    kv_bias = jnp.where(
        is_key,
        jnp.concatenate([keyvalue_bias, mate_bias]),
        jnp.concatenate([mate_bias, keyvalue_bias]),
    )
    w_joint = gather(jnp.concatenate([query_weight, key_w, value_w], axis=1), "col")
    gain_attn = gather(attention_gain, "col").astype(F32)
    gain_mlp = gather(feedforward_gain, "col").astype(F32)
    w_out = gather(output_weight, "col", 1)
    w_gate = gather(gate_weight, "col")
    w_up = gather(up_weight, "col")
    w_down = gather(down_weight, "col", 1)
    inputs = features_to_tokens(tokens_in).astype(F32)
    inverse_attn = lax.rsqrt(jnp.mean(inputs * inputs, axis=-1, keepdims=True) + epsilon)
    normal_attn = inputs * inverse_attn
    normed = gather((normal_attn * gain_attn).astype(BF), "row")
    joint = dot(normed, w_joint) + jnp.concatenate([query_bias, kv_bias]).astype(F32)
    turned = rotate(joint[:, : wq_width + HEAD], cosine, sine).astype(BF)
    queries = turned[:, :wq_width]
    slots = jnp.concatenate([turned[:, wq_width:], joint[:, wq_width + HEAD :].astype(BF)], axis=1)
    slots_all = gather(slots, "col")
    order = lambda v: jnp.moveaxis(v.reshape(cols, rows, sub, -1), 0, 1).reshape(group, -1)
    slots_all = order(slots_all)
    keys, values = slots_all[:, :HEAD], slots_all[:, HEAD:]
    q_heads = queries.reshape(rows, sub, heads, HEAD)
    scale = HEAD ** (-0.5)

    def block_probs(r):
        limit = (r + 1) * row_tokens
        scores = jnp.einsum(
            "qhd,sd->hqs", q_heads[r], keys[:limit], preferred_element_type=F32
        ) * scale
        mine = slice(r * sub, (r + 1) * sub)
        allowed = (my_segment[mine][:, None] == segment[None, :limit]) & (
            places[None, :limit] <= my_places[mine][:, None]
        )
        scores = jnp.where(allowed[None], scores, masked_score)
        e = jnp.exp(scores - jnp.max(scores, axis=-1, keepdims=True))
        return e / jnp.sum(e, axis=-1, keepdims=True)

    attended = []
    for r in range(rows):
        p = block_probs(r)
        limit = (r + 1) * row_tokens
        attended.append(
            jnp.einsum("hqs,sd->qhd", p.astype(BF), values[:limit], preferred_element_type=F32)
            .astype(BF).reshape(sub, wq_width)
        )
    attended = jnp.concatenate(attended, axis=0)
    middle = inputs + scatter_sum(dot(attended, w_out), "row").astype(F32)
    inverse_mlp = lax.rsqrt(jnp.mean(middle * middle, axis=-1, keepdims=True) + epsilon)
    normal_mlp = middle * inverse_mlp
    normed_mlp = gather((normal_mlp * gain_mlp).astype(BF), "row")
    gate_act = dot(normed_mlp, w_gate)
    up_act = dot(normed_mlp, w_up)
    s = jax.nn.sigmoid(gate_act)
    hidden = (gate_act * s * up_act).astype(BF)
    branch = scatter_sum(dot(hidden, w_down), "row").astype(F32)
    layer_out = tokens_to_features((middle + branch).astype(BF))
    grad_out = features_to_tokens(cotangent)
    grad_out_all = gather(grad_out, "row")
    grad_hidden = dot(grad_out_all, w_down, 1, 1)
    grad_gate = (grad_hidden * up_act * s * (1.0 + gate_act * (1.0 - s))).astype(BF)
    grad_up = (grad_hidden * (gate_act * s)).astype(BF)
    grad_normed_mlp = scatter_sum(
        dot(grad_gate, w_gate, 1, 1) + dot(grad_up, w_up, 1, 1), "row"
    ).astype(F32)
    gw_down = dot(hidden, grad_out_all, 0, 0)
    gw_gate = dot(normed_mlp, grad_gate, 0, 0)
    gw_up = dot(normed_mlp, grad_up, 0, 0)
    back, gain_mlp_part = norm_back(grad_normed_mlp, normal_mlp, inverse_mlp, gain_mlp)
    grad_middle = grad_out.astype(F32) + back
    grad_middle_all = gather(grad_middle.astype(BF), "row")
    grad_heads = dot(grad_middle_all, w_out, 1, 1).astype(BF).reshape(rows, sub, heads, HEAD)
    gw_out = dot(attended, grad_middle_all, 0, 0)
    dq, dk, dv = [], 0.0, 0.0
    for r in range(rows):
        limit = (r + 1) * row_tokens
        p = block_probs(r)
        pad = ((0, group - limit), (0, 0))
        dv = dv + jnp.pad(jnp.einsum(
            "hqs,qhd->sd", p.astype(BF), grad_heads[r], preferred_element_type=F32), pad)
        g = jnp.einsum("qhd,sd->hqs", grad_heads[r], values[:limit], preferred_element_type=F32)
        ds = (p * (g - jnp.sum(p * g, axis=-1, keepdims=True))).astype(BF)
        dq.append(jnp.einsum("hqs,sd->qhd", ds, keys[:limit], preferred_element_type=F32)
                  .reshape(sub, wq_width) * scale)
        dk = dk + jnp.pad(jnp.einsum(
            "hqs,qhd->sd", ds, q_heads[r], preferred_element_type=F32) * scale, pad)
    dq = jnp.concatenate(dq, axis=0)
    dslots = jnp.concatenate([dk, dv], axis=1)
    dslots = jnp.moveaxis(dslots.reshape(rows, cols, sub, -1), 1, 0).reshape(group, -1)
    dslots = scatter_sum(dslots, "col").astype(F32)
    dturned = jnp.concatenate([dq, dslots[:, :HEAD]], axis=1)
    grad_joint = jnp.concatenate(
        [rotate(dturned, cosine, -sine), dslots[:, HEAD:]], axis=1
    ).astype(BF)
    grad_normed = scatter_sum(dot(grad_joint, w_joint, 1, 1), "row").astype(F32)
    gw_joint = dot(normed, grad_joint, 0, 0)
    g_bias = jnp.sum(grad_joint.astype(F32), axis=0)
    back, gain_attn_part = norm_back(grad_normed, normal_attn, inverse_attn, gain_attn)
    input_grad = tokens_to_features((grad_middle + back).astype(BF))
    both = lambda v, dim: scatter_sum(scatter_sum(v, "col", dim), "dp").astype(F32)

    def slot_share(v, axis):
        k, w = v[..., wq_width : wq_width + HEAD], v[..., wq_width + HEAD :]
        got = partner(jnp.where(is_key, w, k).astype(BF), "row", 1)
        return jnp.where(is_key, k, w) + got.astype(F32)

    gw_joint = scatter_sum(gw_joint, "col").astype(F32)
    gw_query = scatter_sum(gw_joint[:, :wq_width], "dp").astype(F32)
    gw_keyvalue = scatter_sum(slot_share(gw_joint, 1), "dp").astype(F32)
    g_bias = lax.psum(g_bias, "col")
    g_qb = lax.psum_scatter(g_bias[:wq_width], "dp", scatter_dimension=0, tiled=True)
    g_kvb = slot_share(g_bias, 0)
    g_kvb = lax.psum_scatter(g_kvb, "dp", scatter_dimension=0, tiled=True)
    gains = lax.psum((gain_attn_part, gain_mlp_part), ("dp", "row", "col"))
    mine = lambda v: lax.dynamic_slice_in_dim(v, col * (v.shape[0] // cols), v.shape[0] // cols)
    return (
        layer_out, input_grad, mine(gains[0]), gw_query, g_qb, gw_keyvalue, g_kvb,
        both(gw_out, 1), mine(gains[1]), both(gw_gate, 0), both(gw_up, 0), both(gw_down, 1),
    )


def solution(mesh):
    return jax.shard_map(
        on_device,
        mesh=mesh,
        in_specs=(
            P(("dp", "row"), "col"), P("dp", None), P("col"), P("col", "row"), P("row"),
            P("col", "row"), P("row"), P("row", "col"), P("col"), P("col", "row"),
            P("col", "row"), P("row", "col"), P(("dp", "row"), "col"),
        ),
        out_specs=(
            P(("dp", "row"), "col"), P(("dp", "row"), "col"), P("col"),
            P(("col", "dp"), "row"), P(("row", "dp")), P(("col", "dp"), "row"),
            P(("row", "dp")), P(("row", "dp"), "col"), P("col"), P(("col", "dp"), "row"),
            P(("col", "dp"), "row"), P(("row", "dp"), "col"),
        ),
        check_vma=False,
    )
```

time: 1530 us -> 1050 us (0.69)
  waiting for transfers between devices: 1190 us -> 677 us
  local copies, waits for them, and re-layouts: 25.9 us -> 69.8 us
  other arithmetic: 56.2 us -> 33.4 us
  starting transfers between devices: 5.07 us -> 20.4 us
    reduce_scatter x16 -> x10, waiting for transfers between devices: 843 us -> 173 us  [scatter_sum(): lax.psum_scatter(value.astype(BF), axis, scatter_dimension=dim, tiled=True)]
    unnamed x24 -> x32, waiting for transfers between devices: 2.08 us -> 196 us
    all_gather x8 -> x10, waiting for transfers between devices: 344 us -> 299 us  [gather(): return lax.all_gather(value, axis, axis=dim, tiled=True)]
    unnamed x83 -> x131, local copies, waits for them, and re-layouts: 12.5 us -> 53.2 us
    dot_general x17 -> x35, matrix products: 144 us -> 138 us  [the longest x15 103 us: dot(): lax.dot_general(a, b, (((ca,), (cb,)), ((), ())), preferred_element_type=...]
    psum x5 -> x2, blocking collectives: 48.7 us -> 47.8 us  [the longest x1 40.2 us: on_device(): gains = lax.psum((gain_attn_part, gain_mlp_part), ('dp', 'row', 'col'))]
  transfers between devices with their start and end apart: 26 -> 33, of which waited for: 25 -> 23; matrix products, arithmetic and copies ran while one was open for 9% -> 15% of each run, Pallas kernels for 0% -> 0%
where the time goes in v1:
time: 1050 us; the launch traced here: 1040 us
  waiting for transfers between devices  677 us (64%)
  matrix products  146 us (14%)
  blocking collectives  75.5 us (7%)
  local copies, waits for them, and re-layouts  69.8 us (7%)
  other arithmetic  33.4 us (3%)
  starting transfers between devices  20.4 us (2%)
  between operations  16.6 us (2%)
    all_gather x10, waiting for transfers between devices, gather(): return lax.all_gather(value, axis, axis=dim, tiled=True)  299 us
    unnamed x32, waiting for transfers between devices  196 us
    reduce_scatter x10, waiting for transfers between devices, scatter_sum(): lax.psum_scatter(value.astype(BF), axis, scatter_dimension=dim, tiled=True)  173 us
    dot_general x15, matrix products, dot(): lax.dot_general(a, b, (((ca,), (cb,)), ((), ())), preferred_element_type=...  103 us
    unnamed x131, local copies, waits for them, and re-layouts  53.2 us
    psum x1, blocking collectives, on_device(): gains = lax.psum((gain_attn_part, gain_mlp_part), ('dp', 'row', 'col'))  40.2 us
  transfers between devices with their start and end apart: 33, of which 23 were waited for; matrix products, arithmetic and copies ran while one was open for 15% of the time, Pallas kernels for 0%

profile of v1, /device:TPU:0, one launch (start us, length us, event | category | flops | bytes accessed | tf_op | source)
XLA Modules:
  0.0 1039.0 jit_solution(7187481983563739588)
XLA Ops:
  32.3 27.6 %all-gather.13.cloned.1.call-done = bf16[512,1536]{1,0:T(8,128)(2,1)} async-done(((bf16[128,1536]{1,0:T(8,128)(2,1)}), bf16[512,1536]{1,0:T(8,128)(2,1)}) %all-gather.13.cloned.1.call-update) | async-done | bytes 1572880 | tf_op jit(solution)/shard_map/all_gather | solution.py:24
  59.9 22.9 %all-gather.15.cloned.1.call-done = bf16[1536,640]{1,0:T(8,128)(2,1)} async-done(((bf16[384,640]{1,0:T(8,128)(2,1)}), bf16[1536,640]{1,0:T(8,128)(2,1)}) %all-gather.15.cloned.1.call-update) | async-done | bytes 1966096 | tf_op jit(solution)/shard_map/all_gather | solution.py:24
  93.7 12.3 %all-gather.17.cloned.1.call-done = bf16[2048,256]{1,0:T(8,128)(2,1)} async-done(((bf16[512,256]{1,0:T(8,128)(2,1)}), bf16[2048,256]{1,0:T(8,128)(2,1)}) %all-gather.17.cloned.1.call-update) | async-done | bytes 1048592 | tf_op jit(solution)/shard_map/all_gather | solution.py:24
  133.6 30.2 %reduce-scatter.29.cloned.1.call-done = bf16[128,1536]{1,0:T(8,128)(2,1)} async-done(((bf16[512,1536]{1,0:T(8,128)(2,1)}), bf16[128,1536]{1,0:T(8,128)(2,1)}) %reduce-scatter.29.cloned.1.call-update) | async-done | bytes 393232 | tf_op jit(solution)/shard_map/reduce_scatter | solution.py:28
  168.5 10.0 all_to_all.20
  180.3 22.9 %all-gather.21.cloned.1.call-done = bf16[512,1536]{1,0:T(8,128)(2,1)} async-done(((bf16[128,1536]{1,0:T(8,128)(2,1)}), bf16[512,1536]{1,0:T(8,128)(2,1)}) %all-gather.21.cloned.1.call-update) | async-done | bytes 1572880 | tf_op jit(solution)/shard_map/all_gather | solution.py:24
  203.1 50.1 %all-gather.23.cloned.1.call-done = bf16[1536,2240]{0,1:T(8,128)(2,1)} async-done(((bf16[384,2240]{0,1:T(8,128)(2,1)}), bf16[1536,2240]{0,1:T(8,128)(2,1)}) %all-gather.23.cloned.1.call-update) | async-done | bytes 6881296 | tf_op jit(solution)/shard_map/all_gather | solution.py:24
  253.2 9.4 fusion.95
  262.6 41.8 %all-gather.25.cloned.1.call-done = bf16[1536,2240]{0,1:T(8,128)(2,1)} async-done(((bf16[384,2240]{0,1:T(8,128)(2,1)}), bf16[1536,2240]{0,1:T(8,128)(2,1)}) %all-gather.25.cloned.1.call-update) | async-done | bytes 6881296 | tf_op jit(solution)/shard_map/all_gather | solution.py:24
  304.5 9.3 fusion.96
  313.8 29.9 %all-gather.29.cloned.1.call-done = bf16[512,1536]{1,0:T(8,128)(2,1)} async-done(((bf16[128,1536]{1,0:T(8,128)(2,1)}), bf16[512,1536]{1,0:T(8,128)(2,1)}) %all-gather.29.cloned.1.call-update) | async-done | bytes 1572880 | tf_op jit(solution)/shard_map/all_gather | solution.py:24
  343.7 49.9 %all-gather.27.cloned.1.call-done = bf16[2240,1536]{1,0:T(8,128)(2,1)} async-done(((bf16[2240,384]{1,0:T(8,128)(2,1)}), bf16[2240,1536]{1,0:T(8,128)(2,1)}) %all-gather.27.cloned.1.call-update) | async-done | bytes 6881296 | tf_op jit(solution)/shard_map/all_gather | solution.py:24
  393.7 13.2 %multiply_convert_fusion = (bf16[512,2240]{0,1:T(8,128)(2,1)S(1)}, bf16[512,2240]{0,1:T(8,128)(2,1)S(1)}, bf16[512,2240]{0,1:T(8,128)(2,1)}) fusion(f32[512,2240]{0,1:T(8,128)} %fusion.95, f32[512,2240]{0,1:T(8,128)} %fusion.96, bf16[512,1536]{1,0:T(8,128)(2,1)} %all-gather.29.cloned.1.call-done, bf16[2240,1536]{1,0:T(8,128)(2,1)} %all-gather.27.cloned.1.call-done), kind=kOutput, calls=%fused_computation.7 | convolution fusion | flops 3540418560 | bytes 24510464 | tf_op jit(solution)/shard_map/dot_general | solution.py:15
  406.9 8.1 fusion.97
  420.3 35.4 %reduce-scatter.33.cloned.1.call-done = bf16[128,1536]{1,0:T(8,128)(2,1)} async-done(((bf16[512,1536]{1,0:T(8,128)(2,1)}), bf16[128,1536]{1,0:T(8,128)(2,1)}) %reduce-scatter.33.cloned.1.call-update) | async-done | bytes 393232 | tf_op jit(solution)/shard_map/reduce_scatter | solution.py:28
  459.2 36.2 %all-gather.31.cloned.1.call-done = bf16[512,1536]{1,0:T(8,128)(2,1)} async-done(((bf16[128,1536]{1,0:T(8,128)(2,1)}), bf16[512,1536]{1,0:T(8,128)(2,1)}) %all-gather.31.cloned.1.call-update) | async-done | bytes 1572880 | tf_op jit(solution)/shard_map/all_gather | solution.py:24
  548.8 10.6 %reduce-scatter.35.cloned.1.call-done = bf16[512,256]{0,1:T(8,128)(2,1)} async-done(((bf16[2048,256]{0,1:T(8,128)(2,1)}), bf16[512,256]{0,1:T(8,128)(2,1)}) %reduce-scatter.35.cloned.1.call-update) | async-done | bytes 262160 | tf_op jit(solution)/shard_map/reduce_scatter | solution.py:28
  569.0 8.9 convolution_convert_fusion.1
  577.9 9.6 copy.252
  587.6 8.6 convolution_convert_fusion
  596.2 10.4 %copy.256 = bf16[1536,2240]{1,0:T(8,128)(2,1)} copy(bf16[1536,2240]{0,1:T(8,128)(2,1)} %convolution_convert_fusion) | data formatting | bytes 13762560
  606.8 8.7 convolution_convert_fusion.2
  615.6 9.9 copy.260
  629.7 10.2 convolution_convert_fusion.5
  650.2 36.9 %reduce-scatter.51.cloned.1.call-done = bf16[384,2240]{1,0:T(8,128)(2,1)} async-done(((bf16[1536,2240]{1,0:T(8,128)(2,1)}), bf16[384,2240]{1,0:T(8,128)(2,1)}) %reduce-scatter.51.cloned.1.call-update) | async-done | bytes 1720336
  687.1 66.0 %reduce-scatter.55.cloned.1.call-done = bf16[384,2240]{1,0:T(8,128)(2,1)} async-done(((bf16[1536,2240]{1,0:T(8,128)(2,1)}), bf16[384,2240]{1,0:T(8,128)(2,1)}) %reduce-scatter.55.cloned.1.call-update) | async-done | bytes 1720336
  753.1 66.2 %reduce-scatter.59.cloned.1.call-done = bf16[384,2240]{1,0:T(8,128)(2,1)} async-done(((bf16[1536,2240]{1,0:T(8,128)(2,1)}), bf16[384,2240]{1,0:T(8,128)(2,1)}) %reduce-scatter.59.cloned.1.call-update) | async-done | bytes 1720336
  823.2 34.3 %reduce-scatter.37.cloned.1.call-done = bf16[128,1536]{1,0:T(8,128)(2,1)} async-done(((bf16[512,1536]{1,0:T(8,128)(2,1)}), bf16[128,1536]{1,0:T(8,128)(2,1)}) %reduce-scatter.37.cloned.1.call-update) | async-done | bytes 393232 | tf_op jit(solution)/shard_map/reduce_scatter | solution.py:28
  858.8 35.7 %reduce-scatter.31.cloned.1.call-done = bf16[128,1536]{1,0:T(8,128)(2,1)} async-done(((bf16[512,1536]{1,0:T(8,128)(2,1)}), bf16[128,1536]{1,0:T(8,128)(2,1)}) %reduce-scatter.31.cloned.1.call-update) | async-done | bytes 393232 | tf_op jit(solution)/shard_map/reduce_scatter | solution.py:28
  925.7 40.2 %all-reduce.8 = (f32[1536]{0:T(1024)S(1)}, f32[1536]{0:T(1024)S(1)}) all-reduce(f32[1536]{0:T(1024)S(1)} %get-tuple-element.62, f32[1536]{0:T(1024)S(1)} %get-tuple-element.60), channel_id=1, replica_groups=mesh['dp'=2,'row'=4,'col'=4] {'dp','row','col'}, use_global_device_ids=true, to_apply=%region_25.26 | all-reduce | flops 3072 | bytes 24576 | tf_op jit(solution)/shard_map/psum | solution.py:210
  973.7 24.2 %reduce-scatter.57.cloned.1.call-done = bf16[192,2240]{1,0:T(8,128)(2,1)} async-done(((bf16[384,2240]{1,0:T(8,128)(2,1)}), bf16[192,2240]{1,0:T(8,128)(2,1)}) %reduce-scatter.57.cloned.1.call-update) | async-done | bytes 860176
  1001.3 27.0 %reduce-scatter.47.cloned.1.call-done = bf16[1120,384]{1,0:T(8,128)(2,1)} async-done(((bf16[2240,384]{1,0:T(8,128)(2,1)}), bf16[1120,384]{1,0:T(8,128)(2,1)}) %reduce-scatter.47.cloned.1.call-update) | async-done | bytes 860176 | tf_op jit(solution)/shard_map/reduce_scatter | solution.py:28
  (321 shorter events, 206.0 us)
Async XLA Ops:
  7.2 12.7 %all-to-all-start = ((bf16[4,128,384]{2,1,0:T(8,128)(2,1)}), bf16[4,128,384]{2,1,0:T(8,128)(2,1)S(1)}, u32[]{:S(2)}, u32[]{:S(2)}) async-start(bf16[4,128,384]{2,1,0:T(8,128)(2,1)} %bitcast.452), calls=%async_computation | async-start | bytes 786432 | tf_op jit(solution)/shard_map/all_to_all | solution.py:34
  11.4 48.5 %all-gather.13.cloned.1.call-start = ((), (), s32[]{:S(2)}) async-start(), calls=%async_computation.20 | async-start | bytes 1966080 | tf_op jit(solution)/shard_map/all_gather | solution.py:24
  21.6 61.1 %all-gather.15.cloned.1.call-start = ((), (), s32[]{:S(2)}) async-start(), calls=%async_computation.21 | async-start | bytes 2457600 | tf_op jit(solution)/shard_map/all_gather | solution.py:24
  21.7 5.6 collective-permute-start
  28.2 77.8 %all-gather.17.cloned.1.call-start = ((), (), s32[]{:S(2)}) async-start(), calls=%async_computation.22 | async-start | bytes 1310720 | tf_op jit(solution)/shard_map/all_gather | solution.py:24
  28.2 4.0 collective-permute-start.1
  89.1 35.8 %all-gather.19.cloned.1.call-start = ((), (), s32[]{:S(2)}) async-start(), calls=%async_computation.23 | async-start | bytes 1474560 | tf_op jit(solution)/shard_map/all_gather | solution.py:24
  89.7 74.1 %reduce-scatter.29.cloned.1.call-start = ((), (), s32[]{:S(2)}) async-start(), calls=%async_computation.24 | async-start | bytes 1966080 | tf_op jit(solution)/shard_map/reduce_scatter | solution.py:28
  128.3 74.8 %all-gather.21.cloned.1.call-start = ((), (), s32[]{:S(2)}) async-start(), calls=%async_computation.25 | async-start | bytes 1966080 | tf_op jit(solution)/shard_map/all_gather | solution.py:24
  166.9 86.3 %all-gather.23.cloned.1.call-start = ((), (), s32[]{:S(2)}) async-start(), calls=%async_computation.26 | async-start | bytes 8601600 | tf_op jit(solution)/shard_map/all_gather | solution.py:24
  167.6 136.8 %all-gather.25.cloned.1.call-start = ((), (), s32[]{:S(2)}) async-start(), calls=%async_computation.27 | async-start | bytes 8601600 | tf_op jit(solution)/shard_map/all_gather | solution.py:24
  168.4 175.4 %all-gather.29.cloned.1.call-start = ((), (), s32[]{:S(2)}) async-start(), calls=%async_computation.30 | async-start | bytes 1966080 | tf_op jit(solution)/shard_map/all_gather | solution.py:24
  179.2 214.4 %all-gather.27.cloned.1.call-start = ((), (), s32[]{:S(2)}) async-start(), calls=%async_computation.28 | async-start | bytes 8601600 | tf_op jit(solution)/shard_map/all_gather | solution.py:24
  179.8 275.8 %reduce-scatter.33.cloned.1.call-start = ((), (), s32[]{:S(2)}) async-start(), calls=%async_computation.31 | async-start | bytes 1966080 | tf_op jit(solution)/shard_map/reduce_scatter | solution.py:28
  420.2 75.2 %all-gather.31.cloned.1.call-start = ((), (), s32[]{:S(2)}) async-start(), calls=%async_computation.32 | async-start | bytes 1966080 | tf_op jit(solution)/shard_map/all_gather | solution.py:24
  459.2 100.2 %reduce-scatter.35.cloned.1.call-start = ((), (), s32[]{:S(2)}) async-start(), calls=%async_computation.33 | async-start | bytes 1310720 | tf_op jit(solution)/shard_map/reduce_scatter | solution.py:28
  535.5 104.5 %reduce-scatter.49.cloned.1.call-start = ((), (), s32[]{:S(2)}) async-start(), calls=%async_computation.40 | async-start | bytes 1474560
  541.5 100.4 %reduce-scatter.39.cloned.1.call-start = ((), (), s32[]{:S(2)}) async-start(), calls=%async_computation.35 | async-start | bytes 2457600 | tf_op jit(solution)/shard_map/reduce_scatter | solution.py:28
  568.9 118.1 %reduce-scatter.51.cloned.1.call-start = ((), (), s32[]{:S(2)}) async-start(), calls=%async_computation.41 | async-start | bytes 8847360
  587.5 165.5 %reduce-scatter.55.cloned.1.call-start = ((), (), s32[]{:S(2)}) async-start(), calls=%async_computation.43 | async-start | bytes 8847360
  606.6 212.7 %reduce-scatter.59.cloned.1.call-start = ((), (), s32[]{:S(2)}) async-start(), calls=%async_computation.45 | async-start | bytes 8847360
  625.5 232.0 %reduce-scatter.37.cloned.1.call-start = ((), (), s32[]{:S(2)}) async-start(), calls=%async_computation.34 | async-start | bytes 1966080 | tf_op jit(solution)/shard_map/reduce_scatter | solution.py:28
  629.7 264.8 %reduce-scatter.31.cloned.1.call-start = ((), (), s32[]{:S(2)}) async-start(), calls=%async_computation.29 | async-start | bytes 1966080 | tf_op jit(solution)/shard_map/reduce_scatter | solution.py:28
  639.9 284.2 %reduce-scatter.45.cloned.1.call-start = ((), (), s32[]{:S(2)}) async-start(), calls=%async_computation.38 | async-start | bytes 442368 | tf_op jit(solution)/shard_map/reduce_scatter | solution.py:28
  641.8 325.4 %reduce-scatter.43.cloned.1.call-start = ((), (), s32[]{:S(2)}) async-start(), calls=%async_computation.37 | async-start | bytes 147456 | tf_op jit(solution)/shard_map/reduce_scatter | solution.py:28
  643.1 5.5 collective-permute-start.2
  649.3 319.4 %reduce-scatter.41.cloned.1.call-start = ((), (), s32[]{:S(2)}) async-start(), calls=%async_computation.36 | async-start | bytes 442368 | tf_op jit(solution)/shard_map/reduce_scatter | solution.py:28
  650.1 320.2 %reduce-scatter.53.cloned.1.call-start = ((), (), s32[]{:S(2)}) async-start(), calls=%async_computation.42 | async-start | bytes 2654208
  687.0 310.9 %reduce-scatter.57.cloned.1.call-start = ((), (), s32[]{:S(2)}) async-start(), calls=%async_computation.44 | async-start | bytes 2654208
  753.1 275.2 %reduce-scatter.47.cloned.1.call-start = ((), (), s32[]{:S(2)}) async-start(), calls=%async_computation.39 | async-start | bytes 2580480 | tf_op jit(solution)/shard_map/reduce_scatter | solution.py:28
  897.0 13.9 %all-to-all-start.1 = ((bf16[4,128,384]{2,1,0:T(8,128)(2,1)}), bf16[4,128,384]{2,1,0:T(8,128)(2,1)S(1)}, u32[]{:S(2)}, u32[]{:S(2)}) async-start(bf16[4,128,384]{2,1,0:T(8,128)(2,1)} %bitcast.394), calls=%async_computation.3 | async-start | bytes 786432 | tf_op jit(solution)/shard_map/all_to_all | solution.py:42
  910.9 56.4 %all-to-all-start.3 = ((bf16[4,128,384]{2,1,0:T(8,128)(2,1)}), bf16[4,128,384]{2,1,0:T(8,128)(2,1)S(1)}, u32[]{:S(2)}, u32[]{:S(2)}) async-start(bf16[4,128,384]{2,1,0:T(8,128)(2,1)} %bitcast.392), calls=%async_computation.8 | async-start | bytes 786432 | tf_op jit(solution)/shard_map/all_to_all | solution.py:42
  (56 other events, 2023.4 us)
Sparse Core Ops, SparseCore 0:
  21.7 38.0 all-gather.12
  62.0 20.7 all-gather.14
  89.2 16.7 all-gather.16
  107.4 17.4 all-gather.18
  128.5 35.2 reduce-scatter.28
  167.0 36.0 all-gather.20
  204.7 48.4 all-gather.22
  254.8 49.6 all-gather.24
  306.6 37.0 all-gather.28
  345.2 48.4 all-gather.26
  420.3 35.2 reduce-scatter.32
  459.3 36.0 all-gather.30
  535.6 23.7 reduce-scatter.34
  562.0 25.7 reduce-scatter.48
  590.1 30.6 reduce-scatter.38
  623.3 63.6 reduce-scatter.50
  689.4 63.6 reduce-scatter.54
  755.6 63.6 reduce-scatter.58
  822.2 35.2 reduce-scatter.36
  860.2 34.2 reduce-scatter.30
  897.3 10.9 reduce-scatter.44
  911.1 9.9 reduce-scatter.42
  924.0 12.5 reduce-scatter.40
  938.7 28.5 reduce-scatter.52
  969.7 28.1 reduce-scatter.56
  1000.6 27.6 reduce-scatter.46

commit v2 on v1

--- a/solution.py
+++ b/solution.py
@@ -1,6 +1,10 @@
+import functools
+
 import jax
 import jax.numpy as jnp
 from jax import lax
+from jax.experimental import pallas as pl
+from jax.experimental.pallas import tpu as pltpu
 from jax.sharding import PartitionSpec as P
 
 HEAD = 128
@@ -9,10 +13,701 @@
 masked_score = -1e30
 BF = jnp.bfloat16
 F32 = jnp.float32
+MESH = pl.DeviceIdType.MESH
+ANY = pl.BlockSpec(memory_space=pl.ANY)
+VMEM = pl.BlockSpec(memory_space=pltpu.VMEM)
+VMEM_LIMIT = 60 * 2**20
 
 
 def dot(a, b, ca=1, cb=0):
     return lax.dot_general(a, b, (((ca,), (cb,)), ((), ())), preferred_element_type=F32)
+
+
+class Net:
+    def __init__(self, sizes, send, recv, local):
+        self.dp, self.R, self.C = sizes
+        self.d = lax.axis_index("dp")
+        self.r = lax.axis_index("row")
+        self.c = lax.axis_index("col")
+        half = self.dp // 2
+        self.h = self.d // half
+        self.send, self.recv, self.local = send, recv, local
+        self.n = 0
+        self.n_local = 0
+        self.other_h = 1 - self.h
+        self.mate = (lax.rem(self.d + half, self.dp), self.r, self.c)
+        self.sibling = self.at_col(self.c + 1 - 2 * lax.rem(self.c, 2))
+        self.across_c = lax.rem(self.c + 2, 4)
+        self.across = self.at_col(self.across_c)
+
+    def at_col(self, c):
+        return (self.d, self.r, c)
+
+    def at_row(self, r):
+        return (self.d, r, self.c)
+
+    def copy(self, src, dst, dev):
+        i = self.n
+        self.n += 1
+        return pltpu.make_async_remote_copy(
+            src_ref=src, dst_ref=dst, send_sem=self.send.at[i], recv_sem=self.recv.at[i],
+            device_id=dev, device_id_type=MESH,
+        )
+
+    def like(self, copy_index, src, dst, dev):
+        return pltpu.make_async_remote_copy(
+            src_ref=src, dst_ref=dst, send_sem=self.send.at[copy_index],
+            recv_sem=self.recv.at[copy_index], device_id=dev, device_id_type=MESH,
+        )
+
+    def here(self, src, dst):
+        i = self.n_local
+        self.n_local += 1
+        return pltpu.make_async_copy(src, dst, self.local.at[i])
+
+    def barrier(self):
+        sem = pltpu.get_barrier_semaphore()
+        for k in range(1, self.C):
+            pl.semaphore_signal(
+                sem, inc=1, device_id=self.at_col(lax.rem(self.c + k, self.C)), device_id_type=MESH
+            )
+        pl.semaphore_signal(sem, inc=1, device_id=self.mate, device_id_type=MESH)
+
+        @pl.when(self.r > 0)
+        def _():
+            pl.semaphore_signal(sem, inc=1, device_id=self.at_row(self.r - 1), device_id_type=MESH)
+
+        @pl.when(self.r < self.R - 1)
+        def _():
+            pl.semaphore_signal(sem, inc=1, device_id=self.at_row(self.r + 1), device_id_type=MESH)
+
+        count = self.C + (self.r > 0).astype(jnp.int32) + (self.r < self.R - 1).astype(jnp.int32)
+        pl.semaphore_wait(sem, count)
+
+
+class LineGather:
+    def __init__(self, net, buf):
+        self.net, self.buf = net, buf
+        r, R = net.r, net.R
+        self.up_i, self.dn_i = [], []
+        for s in range(R - 1):
+            self.up_i.append(net.n)
+            self.dn_i.append(net.n + 1)
+            net.n += 2
+
+    def _up(self, s, shard):
+        net = self.net
+        b = self.buf.at[jnp.clip(shard, 0, net.R - 1)]
+        return net.like(self.up_i[s], b, b, net.at_row(jnp.minimum(net.r + 1, net.R - 1)))
+
+    def _dn(self, s, shard):
+        net = self.net
+        b = self.buf.at[jnp.clip(shard, 0, net.R - 1)]
+        return net.like(self.dn_i[s], b, b, net.at_row(jnp.maximum(net.r - 1, 0)))
+
+    def step(self, s):
+        net = self.net
+        r, R = net.r, net.R
+        if s > 0:
+
+            @pl.when(r - s >= 0)
+            def _():
+                self._up(s - 1, r - s).wait_recv()
+
+        if s < R - 1:
+
+            @pl.when((r - s >= 0) & (r < R - 1))
+            def _():
+                self._up(s, r - s).start()
+
+        if s > 0:
+
+            @pl.when(r + s < R)
+            def _():
+                self._dn(s - 1, r + s).wait_recv()
+
+        if s < R - 1:
+
+            @pl.when((r + s < R) & (r > 0))
+            def _():
+                self._dn(s, r + s).start()
+
+    def finish(self):
+        net = self.net
+        r, R = net.r, net.R
+        for s in range(R - 1):
+
+            @pl.when((r - s >= 0) & (r < R - 1))
+            def _():
+                self._up(s, r - s).wait_send()
+
+            @pl.when((r + s < R) & (r > 0))
+            def _():
+                self._dn(s, r + s).wait_send()
+
+
+class LineSum:
+    def __init__(self, net, part, from_below, from_above):
+        self.net, self.part, self.bu, self.bd = net, part, from_below, from_above
+        self.base = net.n
+        net.n += 2 * net.R
+
+    def _dn(self, j):
+        net = self.net
+        j = jnp.clip(j, 0, net.R - 1)
+        return net.like(
+            self.base + j, self.part.at[j], self.bd.at[j], net.at_row(jnp.maximum(net.r - 1, 0))
+        )
+
+    def _up(self, j):
+        net = self.net
+        j = jnp.clip(j, 0, net.R - 1)
+        return net.like(
+            self.base + net.R + j, self.part.at[j], self.bu.at[j],
+            net.at_row(jnp.minimum(net.r + 1, net.R - 1)),
+        )
+
+    def _add(self, j, buf):
+        self.part[j] = (self.part[j].astype(F32) + buf[j].astype(F32)).astype(BF)
+
+    def step(self, t):
+        net = self.net
+        r, R = net.r, net.R
+        j = t - (R - 1 - r)
+        k = R - 1 - (t - r)
+
+        @pl.when((j >= 0) & (r < R - 1))
+        def _():
+            self._dn(j).wait_recv()
+
+        @pl.when((j >= 0) & (j < r))
+        def _():
+            @pl.when(r < R - 1)
+            def _():
+                self._add(j, self.bd)
+
+            self._dn(j).start()
+
+        @pl.when((k <= R - 1) & (r > 0))
+        def _():
+            self._up(k).wait_recv()
+
+        @pl.when((k <= R - 1) & (k > r))
+        def _():
+            @pl.when(r > 0)
+            def _():
+                self._add(k, self.bu)
+
+            self._up(k).start()
+
+    def finish(self):
+        net = self.net
+        r, R = net.r, net.R
+        for j in range(R):
+
+            @pl.when(j < r)
+            def _():
+                self._dn(j).wait_send()
+
+            @pl.when(j > r)
+            def _():
+                self._up(j).wait_send()
+
+    def total_into(self, out):
+        net = self.net
+        r, R = net.r, net.R
+        out[...] += self.part[r].astype(F32)
+
+        @pl.when(r < R - 1)
+        def _():
+            out[...] += self.bd[r].astype(F32)
+
+        @pl.when(r > 0)
+        def _():
+            out[...] += self.bu[r].astype(F32)
+
+
+class WeightGather:
+    def __init__(self, net, src, full, by_rows, piece=0, pieces=1):
+        self.net, self.full, self.by_rows = net, full, by_rows
+        if by_rows:
+            self.n, self.w = full.shape[0] // net.C, full.shape[1]
+        else:
+            self.n, self.w = full.shape[0] // pieces, full.shape[1] // net.C
+        self.first = piece * self.n
+        if src is not None:
+            src = src.at[pl.ds(self.first, self.n)]
+        c, p, h, o = net.c, net.across_c, net.h, net.other_h
+        half = self.n // 2
+        self.here = None
+        if src is not None:
+            self.here = net.here(src, self.view(c, 0, 2))
+            own_half = src.at[pl.ds(pl.multiple_of(h * half, 16), half)]
+            own = src
+        else:
+            own_half, own = self.view(c, h, 1), self.view(c, 0, 2)
+        self.x = net.copy(own_half, self.view(c, h, 1), net.across)
+        self.sib = net.copy(own, self.view(c, 0, 2), net.sibling)
+        self.y = net.copy(self.view(p, h, 1), self.view(p, h, 1), net.mate)
+        self.sib_h = net.copy(self.view(p, h, 1), self.view(p, h, 1), net.sibling)
+        self.sib_o = net.copy(self.view(p, o, 1), self.view(p, o, 1), net.sibling)
+
+    def view(self, b, h, halves):
+        half = self.n // 2
+        if self.by_rows:
+            return self.full.at[pl.ds(pl.multiple_of(b * self.n + h * half, 16), halves * half)]
+        return self.full.at[
+            pl.ds(pl.multiple_of(self.first + h * half, 16), halves * half),
+            pl.ds(pl.multiple_of(b * self.w, 128), self.w),
+        ]
+
+    def start(self):
+        if self.here is not None:
+            self.here.start()
+        self.x.start()
+        self.sib.start()
+
+    def pass_x(self):
+        self.x.wait_recv()
+        self.y.start()
+        self.sib_h.start()
+
+    def pass_y(self):
+        self.y.wait_recv()
+        self.sib_o.start()
+
+    def arrive(self):
+        if self.here is not None:
+            self.here.wait()
+        self.sib.wait_recv()
+        self.sib_h.wait_recv()
+        self.sib_o.wait_recv()
+
+    def finish(self):
+        for cp in (self.x, self.sib, self.y, self.sib_h, self.sib_o):
+            cp.wait_send()
+
+
+def turn(values, cos2, sin2):
+    heads = []
+    for i in range(values.shape[1] // HEAD):
+        v = values[:, i * HEAD : (i + 1) * HEAD]
+        heads.append(v * cos2 + pltpu.roll(v, HEAD // 2, 1) * sin2)
+    return jnp.concatenate(heads, axis=1) if len(heads) > 1 else heads[0]
+
+
+def attention_kernel(
+    sizes,
+    tok, cot, wq, wkv, wo, wg, wu, small, qb, kvb, cos2, sin2, qpos,
+    o_mid, o_nmlp, o_gains, o_normed, o_q, o_kv, o_att, o_cot, o_wj, o_wo, o_wg, o_wu,
+    xin, cin, gains, kvb2, nall, call, wj, wov, kv, qs, att, part, rbu, rbd, send, recv, local,
+):
+    net = Net(sizes, send, recv, local)
+    R, C, r, c = net.R, net.C, net.r, net.c
+    sub, width = nall.shape[1], nall.shape[2]
+    block = tok.shape[1]
+    row_tok = sub * C
+    n_tok = sub * R
+    qw = wq.shape[1]
+    slot = lax.rem(r, 2)
+    partner = net.at_row(r + 1 - 2 * slot)
+    net.barrier()
+
+    def spread(src, dst):
+        mine = pl.multiple_of(c * sub, sub)
+        local_copy = net.here(src.at[pl.ds(mine, sub)], dst.at[c])
+        copies = []
+        for k in range(1, C):
+            to = lax.rem(c + k, C)
+            frm = lax.rem(c + C - k, C)
+            i = net.n
+            net.n += 1
+            rows = pl.ds(pl.multiple_of(to * sub, sub), sub)
+            copies.append(
+                (net.like(i, src.at[rows], dst.at[c], net.at_col(to)),
+                 net.like(i, src.at[rows], dst.at[frm], net.at_col(to)))
+            )
+        return local_copy, copies
+
+    def begin(pair):
+        pair[0].start()
+        for out, _ in pair[1]:
+            out.start()
+
+    def arrived(pair):
+        pair[0].wait()
+        for _, inc in pair[1]:
+            inc.wait_recv()
+
+    tok_in, cot_in = spread(tok, xin), spread(cot, cin)
+    begin(tok_in)
+    gain_own = net.here(small, gains.at[c])
+    gain_own.start()
+    gain_copies = []
+    for k in range(1, C):
+        to, frm = lax.rem(c + k, C), lax.rem(c + C - k, C)
+        i = net.n
+        net.n += 1
+        out = net.like(i, small, gains.at[c], net.at_col(to))
+        gain_copies.append((out, net.like(i, small, gains.at[frm], net.at_col(to))))
+        out.start()
+    own_rows = pl.ds(pl.multiple_of(c * block, block), block)
+    col_own = pl.ds(pl.multiple_of(qw + slot * HEAD, HEAD), HEAD)
+    col_mate = pl.ds(pl.multiple_of(qw + (1 - slot) * HEAD, HEAD), HEAD)
+    kv_x = net.copy(wkv, wj.at[own_rows, col_own], partner)
+    kv_in = net.like(net.n - 1, wkv, wj.at[own_rows, col_mate], partner)
+    kv_x.start()
+    kvb_x = net.copy(kvb, kvb2.at[slot], partner)
+    kvb_in = net.like(net.n - 1, kvb, kvb2.at[1 - slot], partner)
+    kvb_x.start()
+    kvb_own = net.here(kvb, kvb2.at[slot])
+    kvb_own.start()
+    wq_own = net.here(wq, wj.at[own_rows, pl.ds(0, qw)])
+    wq_own.start()
+    wkv_own = net.here(wkv, wj.at[own_rows, col_own])
+    wkv_own.start()
+    g_joint = WeightGather(net, None, wj, True)
+    g_out = WeightGather(net, wo, wov, False)
+    bulk = [WeightGather(net, w, o, False, i, 2) for w, o in ((wg, o_wg), (wu, o_wu)) for i in (0, 1)]
+
+    arrived(tok_in)
+    gain_own.wait()
+    for _, inc in gain_copies:
+        inc.wait_recv()
+    for k in range(C):
+        o_gains[:, k * block : (k + 1) * block] = gains[k, :, :block]
+        o_gains[:, width + k * block : width + (k + 1) * block] = gains[k, :, block:]
+    x = jnp.concatenate([xin[k].astype(F32) for k in range(C)], axis=1)
+    o_mid[...] = x
+    inv = lax.rsqrt(jnp.mean(x * x, axis=-1, keepdims=True) + epsilon)
+    nall[r] = (x * inv * o_gains[0:1, :width]).astype(BF)
+    g_n = LineGather(net, nall)
+    g_n.step(0)
+    wq_own.wait()
+    wkv_own.wait()
+    kv_in.wait_recv()
+    g_joint.start()
+    g_out.start()
+    begin(cot_in)
+    g_joint.pass_x()
+    g_out.pass_x()
+    bulk[0].start()
+    g_joint.pass_y()
+    g_n.step(1)
+    g_out.pass_y()
+    bulk[1].start()
+    arrived(cot_in)
+    for k in range(C):
+        call[r, :, k * block : (k + 1) * block] = cin[k]
+    g_n.step(2)
+    bulk[0].pass_x()
+    g_joint.arrive()
+    kvb_own.wait()
+    kvb_in.wait_recv()
+    g_n.step(3)
+    g_cot = LineGather(net, call)
+    g_cot.step(0)
+    bias = jnp.concatenate([qb[0:1, :], kvb2[0, 0:1, :], kvb2[1, 0:1, :]], axis=1)
+    joint = dot(nall[...].reshape(n_tok, width), wj[...]) + bias
+    key = turn(joint[:, qw : qw + HEAD], cos2[...], sin2[...]).astype(BF)
+    kv[:, c, :, :HEAD] = key.reshape(R, sub, HEAD)
+    kv[:, c, :, HEAD:] = joint[:, qw + HEAD :].astype(BF).reshape(R, sub, HEAD)
+    kv_copies = []
+    for k in range(1, C):
+        to, frm = lax.rem(c + k, C), lax.rem(c + C - k, C)
+        i = net.n
+        net.n += 1
+        out = net.like(i, kv.at[:, c], kv.at[:, c], net.at_col(to))
+        kv_copies.append((out, net.like(i, kv.at[:, frm], kv.at[:, frm], net.at_col(to))))
+        out.start()
+    qs[...] = turn(joint[:, :qw], cos2[...], sin2[...]).astype(BF)
+    out_normed = net.here(nall, o_normed)
+    out_normed.start()
+    out_wj = net.here(wj, o_wj)
+    out_wj.start()
+    for _, inc in kv_copies:
+        inc.wait_recv()
+    bulk[1].pass_x()
+    bulk[2].start()
+    bulk[3].start()
+    bulk[0].pass_y()
+    g_cot.step(1)
+    out_kv = net.here(kv, o_kv)
+    out_kv.start()
+    scale = HEAD ** (-0.5)
+    for rr in range(R):
+        limit = (rr + 1) * row_tok
+        keys = kv[: rr + 1, :, :, :HEAD].reshape(limit, HEAD)
+        values = kv[: rr + 1, :, :, HEAD:].reshape(limit, HEAD)
+        mine = slice(rr * sub, (rr + 1) * sub)
+        place = lax.broadcasted_iota(jnp.int32, (sub, limit), 1)
+        allowed = (place >= qpos[mine, 0:1]) & (place <= qpos[mine, 1:2])
+        for h in range(qw // HEAD):
+            cols = slice(h * HEAD, (h + 1) * HEAD)
+            s = jnp.where(allowed, dot(qs[mine, cols], keys, 1, 1) * scale, masked_score)
+            e = jnp.exp(s - jnp.max(s, axis=-1, keepdims=True))
+            p = e * (1.0 / jnp.sum(e, axis=-1, keepdims=True))
+            att[mine, cols] = dot(p.astype(BF), values).astype(BF)
+    g_out.arrive()
+    part[...] = dot(att[...], wov[...]).astype(BF).reshape(R, sub, width)
+    rs = LineSum(net, part, rbu, rbd)
+    rs.step(0)
+    out_q = net.here(qs, o_q)
+    out_q.start()
+    out_att = net.here(att, o_att)
+    out_att.start()
+    out_wo = net.here(wov, o_wo)
+    out_wo.start()
+    g_cot.step(2)
+    bulk[1].pass_y()
+    bulk[2].pass_x()
+    rs.step(1)
+    g_cot.step(3)
+    out_cot = net.here(call, o_cot)
+    out_cot.start()
+    bulk[3].pass_x()
+    rs.step(2)
+    bulk[2].pass_y()
+    rs.step(3)
+    rs.total_into(o_mid)
+    mid = o_mid[...]
+    inv = lax.rsqrt(jnp.mean(mid * mid, axis=-1, keepdims=True) + epsilon)
+    o_nmlp[...] = (mid * inv * o_gains[0:1, width:]).astype(BF)
+    bulk[3].pass_y()
+    for g in bulk:
+        g.arrive()
+    for g in [g_joint, g_out, g_n, g_cot, rs] + bulk:
+        g.finish()
+    for out, _ in tok_in[1] + cot_in[1] + gain_copies + kv_copies:
+        out.wait_send()
+    kv_x.wait_send()
+    kvb_x.wait_send()
+    for cp in (out_normed, out_wj, out_kv, out_q, out_att, out_wo, out_cot):
+        cp.wait()
+
+
+def attention_forward(sizes, tok, cot, wq, wkv, wo, wg, wu, small, qb, kvb, cos2, sin2, qpos):
+    dp, R, C = sizes
+    sub = tok.shape[0] // C
+    block = tok.shape[1]
+    width = block * C
+    qw, jw = wq.shape[1], wq.shape[1] + 2 * HEAD
+    n = sub * R
+    ff = wg.shape[0]
+    shape = jax.ShapeDtypeStruct
+    outs = [
+        (shape((sub, width), F32), VMEM), (shape((sub, width), BF), VMEM),
+        (shape((8, 2 * width), F32), VMEM), (shape((R, sub, width), BF), ANY),
+        (shape((n, qw), BF), ANY), (shape((R, C, sub, 2 * HEAD), BF), ANY),
+        (shape((n, qw), BF), ANY), (shape((R, sub, width), BF), ANY),
+        (shape((width, jw), BF), ANY), (shape((qw, width), BF), ANY),
+        (shape((ff, width), BF), ANY), (shape((ff, width), BF), ANY),
+    ]
+    return pl.pallas_call(
+        functools.partial(attention_kernel, sizes),
+        out_shape=[o for o, _ in outs],
+        in_specs=[ANY] * 7 + [VMEM] * 6,
+        out_specs=[s for _, s in outs],
+        scratch_shapes=[
+            pltpu.VMEM((C, sub, block), BF), pltpu.VMEM((C, sub, block), BF),
+            pltpu.VMEM((C, 8, 2 * block), F32), pltpu.VMEM((2, 8, HEAD), F32),
+            pltpu.VMEM((R, sub, width), BF), pltpu.VMEM((R, sub, width), BF),
+            pltpu.VMEM((width, jw), BF), pltpu.VMEM((qw, width), BF),
+            pltpu.VMEM((R, C, sub, 2 * HEAD), BF), pltpu.VMEM((n, qw), BF),
+            pltpu.VMEM((n, qw), BF), pltpu.VMEM((R, sub, width), BF),
+            pltpu.VMEM((R, sub, width), BF), pltpu.VMEM((R, sub, width), BF),
+            pltpu.SemaphoreType.DMA((64,)), pltpu.SemaphoreType.DMA((64,)),
+            pltpu.SemaphoreType.DMA((24,)),
+        ],
+        compiler_params=pltpu.CompilerParams(
+            collective_id=1, has_side_effects=True, vmem_limit_bytes=VMEM_LIMIT
+        ),
+        name="attention_forward",
+    )(tok, cot, wq, wkv, wo, wg, wu, small, qb, kvb, cos2, sin2, qpos)
+
+
+def feedforward_kernel(
+    sizes,
+    nmlp, mid, gains, cot, wg, wu, wd,
+    o_gmid, o_gain, o_down, o_sum,
+    w_gate, w_up, w_down, xall, call, gh, hid, gg, gu, gh_r, hid_r, gg_r, gu_r, acc, part, rbu, rbd, rx,
+    send, recv, local,
+):
+    net = Net(sizes, send, recv, local)
+    R, C, r, c = net.R, net.C, net.r, net.c
+    sub, width = nmlp.shape
+    n_tok = sub * R
+    ff = w_gate.shape[0]
+    tile = hid.shape[2]
+    tiles = hid.shape[0]
+    rest = hid_r.shape[1]
+    g_down = WeightGather(net, wd, w_down, False)
+    in_cot = net.here(cot, call)
+    in_gate = net.here(wg, w_gate)
+    in_up = net.here(wu, w_up)
+    for cp in (in_cot, in_gate, in_up):
+        cp.start()
+    net.barrier()
+    xall[r] = nmlp[...]
+    g_x = LineGather(net, xall)
+    g_x.step(0)
+    g_down.start()
+    g_x.step(1)
+    g_down.pass_x()
+    in_cot.wait()
+    in_gate.wait()
+    in_up.wait()
+    g_x.step(2)
+    g_down.pass_y()
+    g_down.arrive()
+    cot2 = call[...].reshape(n_tok, width)
+
+    def back_tile(rows):
+        return dot(call[...].reshape(n_tok, width), w_down[rows, :], 1, 1)
+
+    def all_tiles(body):
+        @pl.loop(0, tiles)
+        def _(t):
+            body(t, pl.ds(pl.multiple_of(t * tile, 16), tile), gh.at[t], hid.at[t], gg.at[t], gu.at[t])
+
+        body(tiles, pl.ds(tiles * tile, rest), gh_r, hid_r, gg_r, gu_r)
+
+    def hidden_back(t, rows, gh_t, hid_t, gg_t, gu_t):
+        gh_t[...] = back_tile(rows)
+
+    all_tiles(hidden_back)
+    g_x.step(3)
+
+    def act(t, rows, gh_t, hid_t, gg_t, gu_t):
+        x = xall[...].reshape(n_tok, width)
+        gate = dot(x, w_gate[rows, :], 1, 1)
+        up = dot(x, w_up[rows, :], 1, 1)
+        s = jax.nn.sigmoid(gate)
+        silu = gate * s
+        back = gh_t[...]
+        hid_t[...] = (silu * up).astype(BF)
+        gg_t[...] = (back * up * s * (1.0 + gate * (1.0 - s))).astype(BF)
+        gu_t[...] = (back * silu).astype(BF)
+
+    all_tiles(act)
+    acc[...] = jnp.zeros_like(acc)
+
+    def input_back(t, rows, gh_t, hid_t, gg_t, gu_t):
+        acc[...] += dot(gg_t[...], w_gate[rows, :]) + dot(gu_t[...], w_up[rows, :])
+
+    all_tiles(input_back)
+    part[...] = acc[...].astype(BF).reshape(R, sub, width)
+    rs = LineSum(net, part, rbu, rbd)
+    rs.step(0)
+    acc[...] = jnp.zeros_like(acc)
+
+    def down(t, rows, gh_t, hid_t, gg_t, gu_t):
+        acc[...] += dot(hid_t[...], w_down[rows, :])
+
+    all_tiles(down)
+    xall_done = g_x
+    xall_done.finish()
+    g_down.finish()
+    rs.step(1)
+    exchange = []
+
+    def hand_over(m, w):
+        for i, b in enumerate((net.c + 1 - 2 * lax.rem(net.c, 2), lax.rem(net.across_c + 1 - 2 * lax.rem(net.across_c, 2), 4))):
+            cp = net.copy(w.at[:, pl.ds(pl.multiple_of(b * (width // C), 128), width // C)], rx.at[m, i], net.sibling)
+            cp.start()
+            exchange.append(cp)
+
+    def grad_down(t, rows, gh_t, hid_t, gg_t, gu_t):
+        w_down[rows, :] = dot(hid_t[...], call[...].reshape(n_tok, width), 0, 0).astype(BF)
+
+    all_tiles(grad_down)
+    hand_over(0, w_down)
+    rs.step(2)
+
+    def grad_gate(t, rows, gh_t, hid_t, gg_t, gu_t):
+        w_gate[rows, :] = dot(gg_t[...], xall[...].reshape(n_tok, width), 0, 0).astype(BF)
+
+    all_tiles(grad_gate)
+    hand_over(1, w_gate)
+
+    def grad_up(t, rows, gh_t, hid_t, gg_t, gu_t):
+        w_up[rows, :] = dot(gu_t[...], xall[...].reshape(n_tok, width), 0, 0).astype(BF)
+
+    all_tiles(grad_up)
+    hand_over(2, w_up)
+    rs.step(3)
+    o_gmid[...] = jnp.zeros_like(o_gmid)
+    rs.total_into(o_gmid)
+    grad = o_gmid[...]
+    m = mid[...]
+    inv = lax.rsqrt(jnp.mean(m * m, axis=-1, keepdims=True) + epsilon)
+    normal = m * inv
+    e = grad * gains[0:1, width:]
+    back = inv * (e - normal * jnp.mean(e * normal, axis=-1, keepdims=True))
+    o_gain[...] = jnp.broadcast_to(jnp.sum(grad * normal, axis=0, keepdims=True), o_gain.shape)
+    o_gmid[...] = call[r].astype(F32) + back
+    rs.finish()
+    part[...] = acc[...].astype(BF).reshape(R, sub, width)
+    out_down = net.here(part, o_down)
+    out_down.start()
+    outs = []
+    w = width // C
+    for m_i, wref in enumerate((w_down, w_gate, w_up)):
+        for i, b in enumerate((c, net.across_c)):
+            exchange[2 * m_i + i].wait_recv()
+            n_chunk = 5
+            rows_n = ff // n_chunk
+
+            @pl.loop(0, n_chunk)
+            def _(q):
+                rows = pl.ds(pl.multiple_of(q * rows_n, 16), rows_n)
+                mine = wref[rows, pl.ds(pl.multiple_of(b * w, 128), w)]
+                rx[m_i, i, rows, :] = (mine.astype(F32) + rx[m_i, i, rows, :].astype(F32)).astype(BF)
+
+            cp = net.here(rx.at[m_i, i], o_sum.at[m_i, i])
+            cp.start()
+            outs.append(cp)
+    for cp in exchange:
+        cp.wait_send()
+    for cp in outs + [out_down]:
+        cp.wait()
+
+
+def feedforward(sizes, nmlp, mid, gains, cot, wg, wu, wd):
+    dp, R, C = sizes
+    sub, width = nmlp.shape
+    n = R * sub
+    ff = wd.shape[0]
+    tile = 512
+    tiles, rest = ff // tile, ff % tile
+    shape = jax.ShapeDtypeStruct
+    outs = [
+        (shape((sub, width), F32), VMEM), (shape((8, width), F32), VMEM),
+        (shape((R, sub, width), BF), ANY), (shape((3, 2, ff, width // C), BF), ANY),
+    ]
+    return pl.pallas_call(
+        functools.partial(feedforward_kernel, sizes),
+        out_shape=[o for o, _ in outs],
+        in_specs=[VMEM, VMEM, VMEM, ANY, ANY, ANY, ANY],
+        out_specs=[s for _, s in outs],
+        scratch_shapes=[
+            pltpu.VMEM((ff, width), BF), pltpu.VMEM((ff, width), BF), pltpu.VMEM((ff, width), BF),
+            pltpu.VMEM((R, sub, width), BF), pltpu.VMEM((R, sub, width), BF),
+            pltpu.VMEM((tiles, n, tile), F32), pltpu.VMEM((tiles, n, tile), BF),
+            pltpu.VMEM((tiles, n, tile), BF), pltpu.VMEM((tiles, n, tile), BF),
+            pltpu.VMEM((n, rest), F32), pltpu.VMEM((n, rest), BF),
+            pltpu.VMEM((n, rest), BF), pltpu.VMEM((n, rest), BF),
+            pltpu.VMEM((n, width), F32), pltpu.VMEM((R, sub, width), BF),
+            pltpu.VMEM((R, sub, width), BF), pltpu.VMEM((R, sub, width), BF),
+            pltpu.VMEM((3, 2, ff, width // C), BF),
+            pltpu.SemaphoreType.DMA((48,)), pltpu.SemaphoreType.DMA((48,)),
+            pltpu.SemaphoreType.DMA((24,)),
+        ],
+        compiler_params=pltpu.CompilerParams(
+            collective_id=2, has_side_effects=True, vmem_limit_bytes=VMEM_LIMIT
+        ),
+        name="feedforward",
+    )(nmlp, mid, gains, cot, wg, wu, wd)
 
 
 def partner(value, axis, mask):
@@ -78,44 +773,35 @@
     wq_width = query_weight.shape[1]
     heads = wq_width // HEAD
     is_key = lax.axis_index("row") % 2 == 0
+    sizes = (lax.axis_size("dp"), rows, cols)
+    width = tokens_in.shape[1] * cols
     places = jnp.arange(group, dtype=jnp.int32)
-    lengths = seq_lengths[0]
-    ends = jnp.cumsum(lengths)
-    segment = jnp.sum((places[:, None] >= ends[None, :]).astype(jnp.int32), axis=1)
-    owners = segment[:, None] == jnp.arange(lengths.shape[0], dtype=jnp.int32)[None, :]
-    first = jnp.sum(jnp.where(owners, (ends - lengths)[None, :], 0), axis=1)
-    positions = places - first
+    ends = jnp.cumsum(seq_lengths[0])
+    first = jnp.max(jnp.where(places[:, None] >= ends[None, :-1], ends[None, :-1], 0), axis=1)
     own = lambda v: lax.dynamic_slice_in_dim(v.reshape(rows, cols, sub), col, 1, 1).reshape(-1)
-    my_places, my_segment, my_positions = own(places), own(segment), own(positions)
-    cosine, sine = rotation(my_positions)
-    mate = partner(keyvalue_weight, "row", 1)
-    mate_bias = partner(keyvalue_bias, "row", 1)
-    key_w = jnp.where(is_key, keyvalue_weight, mate)
-    value_w = jnp.where(is_key, mate, keyvalue_weight)
-    kv_bias = jnp.where(
-        is_key,
-        jnp.concatenate([keyvalue_bias, mate_bias]),
-        jnp.concatenate([mate_bias, keyvalue_bias]),
+    my_places, my_first = own(places), own(first)
+    cosine, sine = rotation(my_places - my_first)
+    cos2 = jnp.concatenate([cosine, cosine], axis=1)
+    sin2 = jnp.concatenate([-sine, sine], axis=1)
+    qpos = jnp.stack([my_first, my_places], axis=1)
+    wide = lambda v: jnp.broadcast_to(v.astype(F32)[None], (8, v.shape[0]))
+    small = wide(jnp.concatenate([attention_gain, feedforward_gain]))
+    (middle, nmlp, gains_all, normed, queries, kv, attended, grad_out_all, w_joint, w_out,
+     w_gate, w_up) = attention_forward(
+        sizes, tokens_in, cotangent, query_weight, keyvalue_weight, output_weight, gate_weight.T,
+        up_weight.T, small, wide(query_bias), wide(keyvalue_bias), cos2, sin2, qpos,
     )
-    w_joint = gather(jnp.concatenate([query_weight, key_w, value_w], axis=1), "col")
-    gain_attn = gather(attention_gain, "col").astype(F32)
-    gain_mlp = gather(feedforward_gain, "col").astype(F32)
-    w_out = gather(output_weight, "col", 1)
-    w_gate = gather(gate_weight, "col")
-    w_up = gather(up_weight, "col")
-    w_down = gather(down_weight, "col", 1)
+    grad_middle, gain_mlp_part, down_part, block_sums = feedforward(
+        sizes, nmlp, middle, gains_all, grad_out_all, w_gate, w_up, down_weight
+    )
+    gain_mlp_part = gain_mlp_part[0]
+    gain_attn, gain_mlp = gains_all[0, :width], gains_all[0, width:]
     inputs = features_to_tokens(tokens_in).astype(F32)
     inverse_attn = lax.rsqrt(jnp.mean(inputs * inputs, axis=-1, keepdims=True) + epsilon)
     normal_attn = inputs * inverse_attn
-    normed = gather((normal_attn * gain_attn).astype(BF), "row")
-    joint = dot(normed, w_joint) + jnp.concatenate([query_bias, kv_bias]).astype(F32)
-    turned = rotate(joint[:, : wq_width + HEAD], cosine, sine).astype(BF)
-    queries = turned[:, :wq_width]
-    slots = jnp.concatenate([turned[:, wq_width:], joint[:, wq_width + HEAD :].astype(BF)], axis=1)
-    slots_all = gather(slots, "col")
-    order = lambda v: jnp.moveaxis(v.reshape(cols, rows, sub, -1), 0, 1).reshape(group, -1)
-    slots_all = order(slots_all)
-    keys, values = slots_all[:, :HEAD], slots_all[:, HEAD:]
+    normed = normed.reshape(-1, width)
+    keys = kv[..., :HEAD].reshape(group, HEAD)
+    values = kv[..., HEAD:].reshape(group, HEAD)
     q_heads = queries.reshape(rows, sub, heads, HEAD)
     scale = HEAD ** (-0.5)
 
@@ -125,45 +811,15 @@
             "qhd,sd->hqs", q_heads[r], keys[:limit], preferred_element_type=F32
         ) * scale
         mine = slice(r * sub, (r + 1) * sub)
-        allowed = (my_segment[mine][:, None] == segment[None, :limit]) & (
+        allowed = (places[None, :limit] >= my_first[mine][:, None]) & (
             places[None, :limit] <= my_places[mine][:, None]
         )
         scores = jnp.where(allowed[None], scores, masked_score)
         e = jnp.exp(scores - jnp.max(scores, axis=-1, keepdims=True))
         return e / jnp.sum(e, axis=-1, keepdims=True)
 
-    attended = []
-    for r in range(rows):
-        p = block_probs(r)
-        limit = (r + 1) * row_tokens
-        attended.append(
-            jnp.einsum("hqs,sd->qhd", p.astype(BF), values[:limit], preferred_element_type=F32)
-            .astype(BF).reshape(sub, wq_width)
-        )
-    attended = jnp.concatenate(attended, axis=0)
-    middle = inputs + scatter_sum(dot(attended, w_out), "row").astype(F32)
-    inverse_mlp = lax.rsqrt(jnp.mean(middle * middle, axis=-1, keepdims=True) + epsilon)
-    normal_mlp = middle * inverse_mlp
-    normed_mlp = gather((normal_mlp * gain_mlp).astype(BF), "row")
-    gate_act = dot(normed_mlp, w_gate)
-    up_act = dot(normed_mlp, w_up)
-    s = jax.nn.sigmoid(gate_act)
-    hidden = (gate_act * s * up_act).astype(BF)
-    branch = scatter_sum(dot(hidden, w_down), "row").astype(F32)
+    branch = scatter_sum(down_part.reshape(-1, width), "row").astype(F32)
     layer_out = tokens_to_features((middle + branch).astype(BF))
-    grad_out = features_to_tokens(cotangent)
-    grad_out_all = gather(grad_out, "row")
-    grad_hidden = dot(grad_out_all, w_down, 1, 1)
-    grad_gate = (grad_hidden * up_act * s * (1.0 + gate_act * (1.0 - s))).astype(BF)
-    grad_up = (grad_hidden * (gate_act * s)).astype(BF)
-    grad_normed_mlp = scatter_sum(
-        dot(grad_gate, w_gate, 1, 1) + dot(grad_up, w_up, 1, 1), "row"
-    ).astype(F32)
-    gw_down = dot(hidden, grad_out_all, 0, 0)
-    gw_gate = dot(normed_mlp, grad_gate, 0, 0)
-    gw_up = dot(normed_mlp, grad_up, 0, 0)
-    back, gain_mlp_part = norm_back(grad_normed_mlp, normal_mlp, inverse_mlp, gain_mlp)
-    grad_middle = grad_out.astype(F32) + back
     grad_middle_all = gather(grad_middle.astype(BF), "row")
     grad_heads = dot(grad_middle_all, w_out, 1, 1).astype(BF).reshape(rows, sub, heads, HEAD)
     gw_out = dot(attended, grad_middle_all, 0, 0)
@@ -193,6 +849,11 @@
     g_bias = jnp.sum(grad_joint.astype(F32), axis=0)
     back, gain_attn_part = norm_back(grad_normed, normal_attn, inverse_attn, gain_attn)
     input_grad = tokens_to_features((grad_middle + back).astype(BF))
+    across = lambda v: lax.ppermute(v, "col", [(k, (k + 2) % 4) for k in range(4)])
+    pair_sum = block_sums[:, 0].astype(F32) + across(block_sums[:, 1]).astype(F32)
+    gw_down = scatter_sum(pair_sum[0], "dp").astype(F32)
+    gw_gate = scatter_sum(pair_sum[1], "dp", 1).astype(F32).T
+    gw_up = scatter_sum(pair_sum[2], "dp", 1).astype(F32).T
     both = lambda v, dim: scatter_sum(scatter_sum(v, "col", dim), "dp").astype(F32)
 
     def slot_share(v, axis):
@@ -211,7 +872,7 @@
     mine = lambda v: lax.dynamic_slice_in_dim(v, col * (v.shape[0] // cols), v.shape[0] // cols)
     return (
         layer_out, input_grad, mine(gains[0]), gw_query, g_qb, gw_keyvalue, g_kvb,
-        both(gw_out, 1), mine(gains[1]), both(gw_gate, 0), both(gw_up, 0), both(gw_down, 1),
+        both(gw_out, 1), mine(gains[1]), gw_gate, gw_up, gw_down,
     )
 
 

time: 1050 us -> 652 us (0.62)
  waiting for transfers between devices: 677 us -> 185 us
  Pallas kernels: 0 us -> 237 us
  matrix products: 146 us -> 49.8 us
  blocking collectives: 75.5 us -> 52.3 us
  local copies, waits for them, and re-layouts: 69.8 us -> 56.3 us
    all_gather x10 -> x1, waiting for transfers between devices: 299 us -> 18.3 us  [gather(): return lax.all_gather(value, axis, axis=dim, tiled=True)]
    pallas_call x0 -> x2, Pallas kernels: none -> 237 us  [the longest x1 130 us: attention_forward(): pl.pallas_call(functools.partial(attention_kernel, sizes), out_shape=[o f...]
    unnamed x32 -> x15, waiting for transfers between devices: 196 us -> 22.8 us
    reduce_scatter x10 -> x8, waiting for transfers between devices: 173 us -> 39.6 us  [scatter_sum(): lax.psum_scatter(value.astype(BF), axis, scatter_dimension=dim, tiled=True)]
    ppermute x0 -> x1, waiting for transfers between devices: none -> 93.1 us  [on_device(): lax.ppermute(v, 'col', [(k, (k + 2) % 4) for k in range(4)])]
    dot_general x15 -> x4, matrix products: 103 us -> 11.2 us  [dot(): lax.dot_general(a, b, (((ca,), (cb,)), ((), ())), preferred_element_type=...]
    unnamed x131 -> x119, local copies, waits for them, and re-layouts: 53.2 us -> 23.4 us
    all_gather x2 -> x0, blocking collectives: 12.8 us -> none  [gather(): return lax.all_gather(value, axis, axis=dim, tiled=True)]
  transfers between devices with their start and end apart: 33 -> 18, of which waited for: 23 -> 9; matrix products, arithmetic and copies ran while one was open for 15% -> 13% of each run, Pallas kernels for 0% -> 0%
where the time goes in v2:
time: 652 us; the launch traced here: 642 us
  Pallas kernels  237 us (36%)
  waiting for transfers between devices  185 us (28%)
  local copies, waits for them, and re-layouts  56.3 us (9%)
  blocking collectives  52.3 us (8%)
  matrix products  49.8 us (8%)
  other arithmetic  31.1 us (5%)
  between operations  16.7 us (3%)
  starting transfers between devices  13.9 us (2%)
    pallas_call x1, Pallas kernels, attention_forward(): pl.pallas_call(functools.partial(attention_kernel, sizes), out_shape=[o f...  130 us
    pallas_call x1, Pallas kernels, feedforward(): pl.pallas_call(functools.partial(feedforward_kernel, sizes), out_shape=[o...  107 us
    ppermute x1, waiting for transfers between devices, on_device(): lax.ppermute(v, 'col', [(k, (k + 2) % 4) for k in range(4)])  93.1 us
    psum x1, blocking collectives, on_device(): gains = lax.psum((gain_attn_part, gain_mlp_part), ('dp', 'row', 'col'))  41.1 us
    reduce_scatter x8, waiting for transfers between devices, scatter_sum(): lax.psum_scatter(value.astype(BF), axis, scatter_dimension=dim, tiled=True)  39.6 us
    unnamed x119, local copies, waits for them, and re-layouts  23.4 us
    unnamed x15, waiting for transfers between devices  22.8 us
    all_gather x1, waiting for transfers between devices, gather(): return lax.all_gather(value, axis, axis=dim, tiled=True)  18.3 us
  transfers between devices with their start and end apart: 18, of which 9 were waited for; matrix products, arithmetic and copies ran while one was open for 13% of the time, Pallas kernels for 0%

profile of v2, /device:TPU:0, one launch (start us, length us, event | category | flops | bytes accessed | tf_op | source)
XLA Modules:
  0.0 641.9 jit_solution(2749842308003302696)
XLA Ops:
  13.7 130.3 %attention_forward.1 = (f32[128,1536]{1,0:T(8,128)}, bf16[128,1536]{1,0:T(8,128)(2,1)}, f32[8,3072]{1,0:T(8,128)}, bf16[4,128,1536]{2,1,0:T(8,128)(2,1)}, bf16[5...) custom-call(bf16[512,384]{1,0:T(8,128)(2,1)} %tok.1, ...), custom_call_target="tpu_custom_call" | custom-call | tf_op jit(solution)/shard_map/attention_forward/pallas_call | solution.py:506
  144.0 106.7 %feedforward.1 = (f32[128,1536]{1,0:T(8,128)}, f32[8,1536]{1,0:T(8,128)}, bf16[4,128,1536]{2,1,0:T(8,128)(2,1)}, bf16[3,2,2240,384]{3,2,1,0:T(8,128)(2,1)}) custom-call(bf16[128,1536]{1,0:T(8,128)(2,1)} %get-tuple-element.29.nmlp, f32[128,1536]{1,0:T(8,128)} %get-tuple-element.28.mid, f32[8,3072]{1,0:T(8,128)} %get-tuple-element.30.gains, ...), custom_call_target="tpu_custom_call" | custom-call | tf_op jit(solution)/shard_map/feedforward/pallas_call | solution.py:688
  266.8 3.9 fusion.77
  270.6 18.3 %all-gather.2.cloned.1.call-done = bf16[512,1536]{1,0:T(8,128)(2,1)} async-done(((bf16[128,1536]{1,0:T(8,128)(2,1)}), bf16[512,1536]{1,0:T(8,128)(2,1)}) %all-gather.2.cloned.1.call-update) | async-done | bytes 1572880 | tf_op jit(solution)/shard_map/all_gather | solution.py:719
  288.9 2.6 convolution_convert_fusion.3
  297.8 2.9 convolution_bitcast_fusion.6
  304.7 3.3 convolution_bitcast_fusion.2
  314.2 4.6 fusion.19
  322.0 2.6 convert_element_type.183
  324.5 2.7 copy.208
  327.2 2.6 convert_element_type.185
  329.9 3.4 convolution_convert_fusion.2
  333.3 2.5 copy.244
  344.8 9.0 %reduce-scatter.20.cloned.1.call-done = bf16[512,256]{0,1:T(8,128)(2,1)} async-done(((bf16[2048,256]{0,1:T(8,128)(2,1)}), bf16[512,256]{0,1:T(8,128)(2,1)}) %reduce-scatter.20.cloned.1.call-update) | async-done | bytes 262160 | tf_op jit(solution)/shard_map/reduce_scatter | solution.py:723
  356.6 2.6 convolution_convert_fusion.1
  359.3 5.3 slice_bitcast_fusion.1
  365.0 2.7 convolution_convert_fusion
  367.8 21.5 %reduce-scatter.34.cloned.1.call-done = bf16[384,384]{1,0:T(8,128)(2,1)} async-done(((bf16[1536,384]{1,0:T(8,128)(2,1)}), bf16[384,384]{1,0:T(8,128)(2,1)}) %reduce-scatter.34.cloned.1.call-update) | async-done | bytes 294928
  391.2 93.1 %collective-permute-done.2 = bf16[3,2240,384]{2,1,0:T(8,128)(2,1)} collective-permute-done((bf16[3,2240,384]{2,1,0:T(8,128)(2,1)}, bf16[3,2240,384]{2,1,0:T(8,128)(2,1)}, u32[]{:S(2)}, u32[]{:S(2)}) %collective-permute-start.2) | collective-permute-done | bytes 5160992 | tf_op jit(solution)/shard_map/ppermute | solution.py:852
  484.3 5.2 fusion.4
  496.6 3.9 all-to-all-start.1
  504.1 3.8 all-to-all-done.1
  510.0 3.5 all-to-all-start
  513.7 7.2 %all-to-all-done = bf16[4,128,384]{2,1,0:T(8,128)(2,1)S(1)} async-done(((bf16[4,128,384]{2,1,0:T(8,128)(2,1)}), bf16[4,128,384]{2,1,0:T(8,128)(2,1)S(1)}, u32[]{:S(2)}, u32[]{:S(2)}) %all-to-all-start) | async-done | bytes 393248 | tf_op jit(solution)/shard_map/all_to_all | solution.py:737
  521.8 6.2 psum.22
  533.8 3.5 all-to-all-start.2
  538.1 4.9 all-reduce.9
  545.9 41.1 %all-reduce.8 = (f32[1536]{0:T(1024)S(1)}, f32[1536]{0:T(1024)S(1)}) all-reduce(f32[1536]{0:T(1024)S(1)} %get-tuple-element.104, f32[1536]{0:T(1024)S(1)} %slice_reduce_fusion), channel_id=1, replica_groups=mesh['dp'=2,'row'=4,'col'=4] {'dp','row','col'}, use_global_device_ids=true, to_apply=%region_20.21 | all-reduce | flops 3072 | bytes 24576 | tf_op jit(solution)/shard_map/psum | solution.py:871
  596.9 7.0 %reduce-scatter.32.cloned.1.call-done = bf16[1120,384]{1,0:T(8,128)(2,1)} async-done(((bf16[2240,384]{1,0:T(8,128)(2,1)}), bf16[1120,384]{1,0:T(8,128)(2,1)}) %reduce-scatter.32.cloned.1.call-update) | async-done | bytes 860176 | tf_op jit(solution)/shard_map/reduce_scatter | solution.py:723
  603.9 2.5 convert_element_type.210
  606.4 10.3 %reduce-scatter.28.cloned.1.call-done = bf16[192,128]{1,0:T(8,128)(2,1)} async-done(((bf16[384,128]{1,0:T(8,128)(2,1)}), bf16[192,128]{1,0:T(8,128)(2,1)}) %reduce-scatter.28.cloned.1.call-update) | async-done | bytes 49168 | tf_op jit(solution)/shard_map/reduce_scatter | solution.py:723
  618.2 13.3 %reduce-scatter.26.cloned.1.call-done = bf16[192,384]{1,0:T(8,128)(2,1)} async-done(((bf16[384,384]{1,0:T(8,128)(2,1)}), bf16[192,384]{1,0:T(8,128)(2,1)}) %reduce-scatter.26.cloned.1.call-update) | async-done | bytes 147472 | tf_op jit(solution)/shard_map/reduce_scatter | solution.py:723
  (244 shorter events, 92.3 us)
Async XLA Ops:
  7.2 281.7 %all-gather.2.cloned.1.call-start = ((), (), s32[]{:S(2)}) async-start(), calls=%async_computation.15 | async-start | bytes 1966080 | tf_op jit(solution)/shard_map/all_gather | solution.py:719
  144.0 109.0 %copy-start = (bf16[4,4,128,256]{3,2,1,0:T(8,128)(2,1)S(1)}, bf16[4,4,128,256]{3,2,1,0:T(8,128)(2,1)}, u32[]{:S(2)}) copy-start(bf16[4,4,128,256]{3,2,1,0:T(8,128)(2,1)} %get-tuple-element.36) | copy-start | bytes 3145732
  252.8 101.0 %reduce-scatter.20.cloned.1.call-start = ((), (), s32[]{:S(2)}) async-start(), calls=%async_computation.16 | async-start | bytes 1310720 | tf_op jit(solution)/shard_map/reduce_scatter | solution.py:723
  259.6 45.1 %copy-start.15 = (bf16[3,4,128,128]{3,2,1,0:T(8,128)(2,1)}, bf16[3,4,128,128]{3,2,1,0:T(8,128)(2,1)S(1)}, u32[]{:S(2)}) copy-start(bf16[3,4,128,128]{3,2,1,0:T(8,128)(2,1)S(1)} %get-tuple-element.120) | copy-start | bytes 1179652
  265.6 42.4 %copy-start.5 = (f32[3,128,1536]{1,2,0:T(8,128)}, f32[3,128,1536]{1,2,0:T(8,128)S(1)}, u32[]{:S(2)}) copy-start(f32[3,128,1536]{1,2,0:T(8,128)S(1)} %get-tuple-element.147) | copy-start | bytes 7077892
  329.9 59.4 %reduce-scatter.34.cloned.1.call-start = ((), (), s32[]{:S(2)}) async-start(), calls=%async_computation.23 | async-start | bytes 1474560
  335.8 172.3 %reduce-scatter.18.cloned.1.call-start = ((), (), s32[]{:S(2)}) async-start(), calls=%async_computation.14 | async-start | bytes 1966080 | tf_op jit(solution)/shard_map/reduce_scatter | solution.py:723
  336.4 193.2 %reduce-scatter.22.cloned.1.call-start = ((), (), s32[]{:S(2)}) async-start(), calls=%async_computation.17 | async-start | bytes 1966080 | tf_op jit(solution)/shard_map/reduce_scatter | solution.py:723
  344.3 10.5 %copy-start.22 = (f32[128,3,128]{2,0,1:T(8,128)S(1)}, f32[128,3,128]{2,0,1:T(8,128)}, u32[]{:S(2)}) copy-start(f32[128,3,128]{2,0,1:T(8,128)} %convolution_multiply_fusion.4) | copy-start | bytes 589828
  344.3 10.5 %copy-start.23 = (f32[128,3,128]{2,0,1:T(8,128)S(1)}, f32[128,3,128]{2,0,1:T(8,128)}, u32[]{:S(2)}) copy-start(f32[128,3,128]{2,0,1:T(8,128)} %convolution_multiply_fusion.3) | copy-start | bytes 589828
  344.8 10.1 %copy-start.25 = (f32[512,64]{0,1:T(8,128)S(1)}, f32[512,64]{0,1:T(8,128)}, u32[]{:S(2)}) copy-start(f32[512,64]{0,1:T(8,128)} %copy.209) | copy-start | bytes 393220
  354.8 10.2 %copy-start.27 = (bf16[512,128]{0,1:T(8,128)(2,1)}, bf16[512,128]{0,1:T(8,128)(2,1)S(1)}, u32[]{:S(2)}) copy-start(bf16[512,128]{0,1:T(8,128)(2,1)S(1)} %get-tuple-element.132) | copy-start | bytes 393220
  359.2 171.7 %reduce-scatter.24.cloned.1.call-start = ((), (), s32[]{:S(2)}) async-start(), calls=%async_computation.18 | async-start | bytes 2457600 | tf_op jit(solution)/shard_map/reduce_scatter | solution.py:723
  364.6 119.7 %collective-permute-start.2 = (bf16[3,2240,384]{2,1,0:T(8,128)(2,1)}, bf16[3,2240,384]{2,1,0:T(8,128)(2,1)}, u32[]{:S(2)}, u32[]{:S(2)}) collective-permute-start(bf16[3,2240,384]{2,1,0:T(8,128)(2,1)} %slice_bitcast_fusion.1), channel_id=1, source_target_pairs={{0,2},{1,3},{2,0},{3,1},{4,6},{5,7},{6,4},{7,5},{8,10},{9,11},{10,... | collective-permute-start | bytes 15482888 | tf_op jit(solution)/shard_map/ppermute | solution.py:852
  367.7 176.5 %reduce-scatter.30.cloned.1.call-start = ((), (), s32[]{:S(2)}) async-start(), calls=%async_computation.21 | async-start | bytes 442368 | tf_op jit(solution)/shard_map/reduce_scatter | solution.py:723
  391.2 198.0 %reduce-scatter.36.cloned.1.call-start = ((), (), s32[]{:S(2)}) async-start(), calls=%async_computation.24 | async-start | bytes 2654208
  493.6 99.5 %reduce-scatter.38.cloned.1.call-start = ((), (), s32[]{:S(2)}) async-start(), calls=%async_computation.25 | async-start | bytes 2654208
  496.0 107.9 %reduce-scatter.32.cloned.1.call-start = ((), (), s32[]{:S(2)}) async-start(), calls=%async_computation.22 | async-start | bytes 2580480 | tf_op jit(solution)/shard_map/reduce_scatter | solution.py:723
  496.6 11.5 %copy-start.4 = (f32[128,1536]{1,0:T(8,128)S(1)}, f32[128,1536]{1,0:T(8,128)}, u32[]{:S(2)}) copy-start(f32[128,1536]{1,0:T(8,128)} %get-tuple-element.28.mid) | copy-start | bytes 2359300
  496.6 11.3 %all-to-all-start.1 = ((bf16[4,128,384]{2,1,0:T(8,128)(2,1)}), bf16[4,128,384]{2,1,0:T(8,128)(2,1)S(1)}, u32[]{:S(2)}, u32[]{:S(2)}) async-start(bf16[4,128,384]{2,1,0:T(8,128)(2,1)} %bitcast.11), calls=%async_computation.2 | async-start | bytes 786432 | tf_op jit(solution)/shard_map/all_to_all | solution.py:729
  508.0 13.6 %copy-start.9 = (bf16[512,4,128]{0,2,1:T(8,128)(2,1)S(1)}, bf16[512,4,128]{0,2,1:T(8,128)(2,1)}, u32[]{:S(2)}) copy-start(bf16[512,4,128]{0,2,1:T(8,128)(2,1)} %copy-done.8) | copy-start | bytes 1572868
  508.1 13.6 %copy-start.28 = (bf16[512,128]{0,1:T(8,128)(2,1)S(1)}, bf16[512,128]{0,1:T(8,128)(2,1)}, u32[]{:S(2)}) copy-start(bf16[512,128]{0,1:T(8,128)(2,1)} %copy-done.27) | copy-start | bytes 393220
  510.0 10.9 %all-to-all-start = ((bf16[4,128,384]{2,1,0:T(8,128)(2,1)}), bf16[4,128,384]{2,1,0:T(8,128)(2,1)S(1)}, u32[]{:S(2)}, u32[]{:S(2)}) async-start(bf16[4,128,384]{2,1,0:T(8,128)(2,1)} %bitcast.284), calls=%async_computation.1 | async-start | bytes 786432 | tf_op jit(solution)/shard_map/all_to_all | solution.py:737
  521.6 11.1 %copy-start.3 = (f32[128,1536]{1,0:T(8,128)S(1)}, f32[128,1536]{1,0:T(8,128)}, u32[]{:S(2)}) copy-start(f32[128,1536]{1,0:T(8,128)} %get-tuple-element.35) | copy-start | bytes 2359300
  528.0 10.0 %collective-permute-start.1 = (bf16[128]{0:T(256)(128)(2,1)S(1)}, bf16[128]{0:T(256)(128)(2,1)S(1)}, u32[]{:S(2)}, u32[]{:S(2)}) collective-permute-start(bf16[128]{0:T(256)(128)(2,1)S(1)} %fusion.48), channel_id=1, source_target_pairs={{0,4},{4,0},{8,12},{12,8},{1,5},{5,1},{9,13},{13,9},{2,6},{6,2},{1... | collective-permute-start | bytes 776 | tf_op jit(solution)/shard_map/ppermute | solution.py:715
  532.1 5.2 collective-permute-start
  533.0 55.3 %copy-start.20 = (bf16[384,640]{1,0:T(8,128)(2,1)S(1)}, bf16[384,640]{1,0:T(8,128)(2,1)}, u32[]{:S(2)}) copy-start(bf16[384,640]{1,0:T(8,128)(2,1)} %reduce-scatter.24.cloned.1.call-done) | copy-start | bytes 1474564
  533.8 54.5 %all-to-all-start.2 = ((bf16[4,128,384]{2,1,0:T(8,128)(2,1)}), bf16[4,128,384]{2,1,0:T(8,128)(2,1)S(1)}, u32[]{:S(2)}, u32[]{:S(2)}) async-start(bf16[4,128,384]{2,1,0:T(8,128)(2,1)} %bitcast.282), calls=%async_computation.5 | async-start | bytes 786432 | tf_op jit(solution)/shard_map/all_to_all | solution.py:737
  537.3 79.5 %reduce-scatter.28.cloned.1.call-start = ((), (), s32[]{:S(2)}) async-start(), calls=%async_computation.20 | async-start | bytes 147456 | tf_op jit(solution)/shard_map/reduce_scatter | solution.py:723
  538.0 93.4 %reduce-scatter.26.cloned.1.call-start = ((), (), s32[]{:S(2)}) async-start(), calls=%async_computation.19 | async-start | bytes 442368 | tf_op jit(solution)/shard_map/reduce_scatter | solution.py:723
  596.9 36.2 %copy-start.14 = (bf16[4,128,384]{2,1,0:T(8,128)(2,1)S(1)}, bf16[4,128,384]{2,1,0:T(8,128)(2,1)}, u32[]{:S(2)}) copy-start(bf16[4,128,384]{2,1,0:T(8,128)(2,1)} %copy-done.13) | copy-start | bytes 1179652
  596.9 36.9 %copy-start.18 = (bf16[4,128,384]{2,1,0:T(8,128)(2,1)S(1)}, bf16[4,128,384]{2,1,0:T(8,128)(2,1)}, u32[]{:S(2)}) copy-start(bf16[4,128,384]{2,1,0:T(8,128)(2,1)} %copy-done.17) | copy-start | bytes 1179652
  (39 other events, 132.8 us)
Sparse Core Ops, SparseCore 0:
  252.9 35.9 all-gather.1
  330.0 23.7 reduce-scatter.19
  357.1 32.1 reduce-scatter.33
  391.5 35.2 reduce-scatter.17
  429.5 34.2 reduce-scatter.21
  466.3 29.5 reduce-scatter.23
  498.7 12.0 reduce-scatter.29
  513.8 28.2 reduce-scatter.35
  544.3 28.9 reduce-scatter.37
  576.0 27.8 reduce-scatter.31
  606.7 9.9 reduce-scatter.27
  619.4 12.0 reduce-scatter.25
